TPU v7x, 32 devices: a whole 2x2x4 slice. The times are simulated.
32 devices in a mesh: dp: 16 (over z, x, core), mp: 2 (over y).
Axes of the slice: x: 2, y: 2, z: 4, core: 2. Of those that a mesh axis runs over, the one named last changes fastest.
Arguments:
- text_in: bfloat16 [24576, 768], P('dp'), may hold values from -6 to 6
- layout_in: bfloat16 [24576, 192], P('dp'), may hold values from -6 to 6
- token_mask: int32 [24576], P('dp'), may hold values 0 or 1
- box_mask: int32 [24576], P('dp'), may hold values from 0 to 1, as said below
- lengths: int32 [48], P('dp'), may hold values from 256 to 512, as said below
- text_mask_vec: bfloat16 [768], replicated, may hold values from -4 to 4
- layout_mask_vec: bfloat16 [192], replicated, may hold values from -4 to 4
- text_qkv: bfloat16 [3, 768, 768], P(None, None, 'mp'), may hold values from -0.21875 to 0.21875
- text_qv_bias: bfloat16 [2, 768], P(None, 'mp'), may hold values from -3 to 3
- text_out_w: bfloat16 [768, 768], P('mp'), may hold values from -0.625 to 0.625
- text_shifts: bfloat16 [4, 768], replicated, may hold values from -3 to 3
- text_gains: bfloat16 [2, 768], replicated, may hold values from 0.099609375 to 1.8984375
- text_up: bfloat16 [768, 3072], P(None, 'mp'), may hold values from -0.21875 to 0.21875
- text_up_bias: bfloat16 [3072], P('mp'), may hold values from -3 to 3
- text_down: bfloat16 [3072, 768], P('mp'), may hold values from -0.109375 to 0.109375
- layout_qkv: bfloat16 [3, 192, 192], P(None, None, 'mp'), may hold values from -0.4375 to 0.4375
- layout_qv_bias: bfloat16 [2, 192], P(None, 'mp'), may hold values from -3 to 3
- layout_out_w: bfloat16 [192, 192], P('mp'), may hold values from -1.25 to 1.25
- layout_shifts: bfloat16 [4, 192], replicated, may hold values from -3 to 3
- layout_gains: bfloat16 [2, 192], replicated, may hold values from 0.099609375 to 1.8984375
- layout_up: bfloat16 [192, 768], P(None, 'mp'), may hold values from -0.4375 to 0.4375
- layout_up_bias: bfloat16 [768], P('mp'), may hold values from -3 to 3
- layout_down: bfloat16 [768, 192], P('mp'), may hold values from -0.21875 to 0.21875
- text_cot: bfloat16 [24576, 768], P('dp'), may hold values from -6 to 6
- layout_cot: bfloat16 [24576, 192], P('dp'), may hold values from -6 to 6
Outputs:
- text_out: float32 [24576, 768], P('dp')
- layout_out: float32 [24576, 192], P('dp')
- text_in_grad: float32 [24576, 768], P('dp')
- layout_in_grad: float32 [24576, 192], P('dp')
- text_mask_vec_grad: float32 [768], replicated
- layout_mask_vec_grad: float32 [192], replicated
- text_qkv_grad: float32 [3, 768, 768], P(None, 'dp', 'mp')
- text_qv_bias_grad: float32 [2, 768], P(None, 'mp')
- text_out_w_grad: float32 [768, 768], P('mp', 'dp')
- text_shifts_grad: float32 [4, 768], replicated
- text_gains_grad: float32 [2, 768], replicated
- text_up_grad: float32 [768, 3072], P('dp', 'mp')
- text_up_bias_grad: float32 [3072], P('mp')
- text_down_grad: float32 [3072, 768], P('mp', 'dp')
- layout_qkv_grad: float32 [3, 192, 192], P(None, None, 'mp')
- layout_qv_bias_grad: float32 [2, 192], P(None, 'mp')
- layout_out_w_grad: float32 [192, 192], P('mp')
- layout_shifts_grad: float32 [4, 192], replicated
- layout_gains_grad: float32 [2, 192], replicated
- layout_up_grad: float32 [192, 768], P(None, 'mp')
- layout_up_bias_grad: float32 [768], P('mp')
- layout_down_grad: float32 [768, 192], P('mp')
Inputs may be any that keep to these rules, and one draw needn't show every extreme that they name: `box_mask`: boxes are masked in aligned runs of 8 tokens (whole regions). `lengths`: each page's unpadded tokens stand at its start; in every draw some page is full.
All inputs are finite; a program needn't handle non-finite values. No bound on the sum of `token_mask` on one device may be relied on, other than what follows from the above.
Results may differ from a plain program's by a relative error of at most 0.012.
The roundings to bfloat16 on the way count: a program that leaves them out, or rounds other values in their place, can miss the bound.
Values sent between devices are 32-bit elements; how exact they have to be, the bound alone decides.
No kernel may reach another device: no remote copies, remote signals or barrier semaphores. Data moves between devices by JAX's collectives and lax.ppermute only.
A program may use at most 256 MiB of HBM per device.

v0:
```python
import math

import jax
import jax.numpy as jnp
from jax import lax
from jax.sharding import PartitionSpec as P

HD = 64
LHD = 16


EPSILON = 1e-05
NEGATIVE = -1000000000.0


def normalize(values, gain_row, offset):
    row_mean = jnp.mean(values, -1, keepdims=True)
    centered = values - row_mean
    inverse = lax.rsqrt(jnp.mean(centered * centered, -1, keepdims=True) + EPSILON)
    unit_rows = centered * inverse
    return (unit_rows * gain_row + offset, unit_rows, inverse)


def norm_back(gradient, unit_rows, inverse, gain_row):
    scaled = gradient * gain_row
    return inverse * (
        scaled
        - jnp.mean(scaled, -1, keepdims=True)
        - unit_rows * jnp.mean(scaled * unit_rows, -1, keepdims=True)
    )


def project(inputs, weight, bias_pair):
    bias_rows = bias_pair.astype(jnp.float32)
    stacked = jnp.stack([bias_rows[0], jnp.zeros_like(bias_rows[0]), bias_rows[1]])
    product = jnp.einsum("nd,cde->cne", inputs, weight, preferred_element_type=jnp.float32)
    return (product + stacked[:, None, :]).astype(jnp.bfloat16)


def split_heads(values, head_width):
    return values.reshape(values.shape[0], values.shape[1] // head_width, head_width)


def combined_scores(text_q, text_k, layout_q, layout_k, valid_keys):
    text_scores = jnp.einsum(
        "qhd,khd->hqk",
        split_heads(text_q, HD),
        split_heads(text_k, HD),
        preferred_element_type=jnp.float32,
    ) / math.sqrt(HD)
    layout_scores = jnp.einsum(
        "qhd,khd->hqk",
        split_heads(layout_q, LHD),
        split_heads(layout_k, LHD),
        preferred_element_type=jnp.float32,
    ) / math.sqrt(LHD)
    return jnp.where(valid_keys[None, None, :], text_scores + layout_scores, NEGATIVE)


def page_forward(page_items):
    text_q, text_k, text_v, layout_q, layout_k, layout_v, valid_keys = page_items
    masked_scores = combined_scores(text_q, text_k, layout_q, layout_k, valid_keys)
    row_top = jnp.max(masked_scores, -1, keepdims=True)
    raised = jnp.exp(masked_scores - row_top)
    row_sums = jnp.sum(raised, -1, keepdims=True)
    weights_low = (raised / row_sums).astype(jnp.bfloat16)
    seq_len = text_q.shape[0]
    text_heads = jnp.einsum(
        "hqk,khd->qhd", weights_low, split_heads(text_v, HD), preferred_element_type=jnp.float32
    )
    layout_heads = jnp.einsum(
        "hqk,khd->qhd", weights_low, split_heads(layout_v, LHD), preferred_element_type=jnp.float32
    )
    return (
        text_heads.reshape(seq_len, -1).astype(jnp.bfloat16),
        layout_heads.reshape(seq_len, -1).astype(jnp.bfloat16),
        (row_top + jnp.log(row_sums))[..., 0],
    )


def page_backward(page_items):
    (
        text_q,
        text_k,
        text_v,
        layout_q,
        layout_k,
        layout_v,
        valid_keys,
        log_total,
        text_dout,
        layout_dout,
    ) = page_items
    masked_scores = combined_scores(text_q, text_k, layout_q, layout_k, valid_keys)
    weights_full = jnp.exp(masked_scores - log_total[..., None])
    weights_low = weights_full.astype(jnp.bfloat16)

    def score_grad(out_grad, values, head_width):
        weight_grad = jnp.einsum(
            "qhd,khd->hqk",
            split_heads(out_grad, head_width),
            split_heads(values, head_width),
            preferred_element_type=jnp.float32,
        )
        return weights_full * (weight_grad - jnp.sum(weights_full * weight_grad, -1, keepdims=True))

    text_dscore = score_grad(text_dout, text_v, HD)
    layout_dscore = score_grad(layout_dout, layout_v, LHD)
    text_round = ((text_dscore + layout_dscore) / math.sqrt(HD)).astype(jnp.bfloat16)
    layout_round = (layout_dscore / math.sqrt(LHD)).astype(jnp.bfloat16)

    def input_grads(score_round, queries, keys_in, out_grad, head_width):
        seq_len = queries.shape[0]
        query_grad = jnp.einsum(
            "hqk,khd->qhd",
            score_round,
            split_heads(keys_in, head_width),
            preferred_element_type=jnp.float32,
        )
        key_grad = jnp.einsum(
            "hqk,qhd->khd",
            score_round,
            split_heads(queries, head_width),
            preferred_element_type=jnp.float32,
        )
        value_grad = jnp.einsum(
            "hqk,qhd->khd",
            weights_low,
            split_heads(out_grad, head_width),
            preferred_element_type=jnp.float32,
        )
        return jnp.stack(
            [
                query_grad.reshape(seq_len, -1),
                key_grad.reshape(seq_len, -1),
                value_grad.reshape(seq_len, -1),
            ]
        ).astype(jnp.bfloat16)

    return (
        input_grads(text_round, text_q, text_k, text_dout, HD),
        input_grads(layout_round, layout_q, layout_k, layout_dout, LHD),
    )


def ffn_back(residual_grad, activated, pre_gelu, hidden_low, up_weight, down_weight):
    grad_low = residual_grad.astype(jnp.bfloat16)
    down_grad = jnp.einsum("nf,nd->fd", activated, grad_low, preferred_element_type=jnp.float32)
    act_grad = jnp.einsum("nd,fd->nf", grad_low, down_weight, preferred_element_type=jnp.float32)
    _, gelu_pull = jax.vjp(lambda values: jax.nn.gelu(values, approximate=False), pre_gelu)
    pre_grad = gelu_pull(act_grad)[0].astype(jnp.bfloat16)
    up_grad = jnp.einsum("nd,nf->df", hidden_low, pre_grad, preferred_element_type=jnp.float32)
    bias_grad = jnp.sum(pre_grad, 0, dtype=jnp.float32)
    hidden_part = jnp.einsum("nf,df->nd", pre_grad, up_weight, preferred_element_type=jnp.float32)
    return (down_grad, up_grad, bias_grad, hidden_part)


def out_back(first_grad, attended, out_weight):
    grad_low = first_grad.astype(jnp.bfloat16)
    weight_grad = jnp.einsum("ne,nd->ed", attended, grad_low, preferred_element_type=jnp.float32)
    attended_grad = jnp.einsum(
        "nd,ed->ne", grad_low, out_weight, preferred_element_type=jnp.float32
    ).astype(jnp.bfloat16)
    return (weight_grad, attended_grad)


def proj_back(inputs, proj_grads, weight):
    weight_grad = jnp.einsum("nd,cne->cde", inputs, proj_grads, preferred_element_type=jnp.float32)
    column_sums = jnp.sum(proj_grads, 1, dtype=jnp.float32)
    bias_grad = jnp.stack([column_sums[0], column_sums[2]])
    input_part = jnp.einsum("cne,cde->nd", proj_grads, weight, preferred_element_type=jnp.float32)
    return (weight_grad, bias_grad, input_part)


def each_stream(function, *columns):
    return tuple((function(*entries) for entries in zip(*columns)))


def matmul(values, weight):
    return jnp.dot(values, weight, preferred_element_type=jnp.float32)


def shards(
    text_in,
    layout_in,
    token_mask,
    box_mask,
    lengths,
    text_mask_vec,
    layout_mask_vec,
    text_qkv,
    text_qv_bias,
    text_out_w,
    text_shifts,
    text_gains,
    text_up,
    text_up_bias,
    text_down,
    layout_qkv,
    layout_qv_bias,
    layout_out_w,
    layout_shifts,
    layout_gains,
    layout_up,
    layout_up_bias,
    layout_down,
    text_cot,
    layout_cot,
):
    row_count = text_in.shape[0]
    page_count = lengths.shape[0]
    seq_len = row_count // page_count
    half_rows = row_count // lax.axis_size("mp")
    first_row = lax.axis_index("mp") * half_rows

    def own_rows(values):
        return lax.dynamic_slice_in_dim(values, first_row, half_rows, 0)

    def paged(values):
        return values.reshape(page_count, seq_len, values.shape[-1])

    flags = (token_mask[:, None] == 1, box_mask[:, None] == 1)
    inputs = each_stream(
        lambda flag_rows, vector, values: jnp.where(flag_rows, vector[None, :], values),
        flags,
        (text_mask_vec, layout_mask_vec),
        (text_in, layout_in),
    )
    qkv_weights = (text_qkv, layout_qkv)
    projected = each_stream(project, inputs, qkv_weights, (text_qv_bias, layout_qv_bias))
    valid_keys = lax.broadcasted_iota(jnp.int32, (page_count, seq_len), 1) < lengths[:, None]
    page_inputs = tuple(
        (paged(stream_proj[which_slot]) for stream_proj in projected for which_slot in range(3))
    ) + (valid_keys,)
    text_att, layout_att, log_total = lax.map(page_forward, page_inputs)
    attended = (text_att.reshape(row_count, -1), layout_att.reshape(row_count, -1))
    out_weights = (text_out_w, layout_out_w)
    partials = each_stream(matmul, attended, out_weights)
    offsets = (text_shifts.astype(jnp.float32), layout_shifts.astype(jnp.float32))
    gain_rows = (text_gains.astype(jnp.float32), layout_gains.astype(jnp.float32))
    bases = each_stream(
        lambda values, offset_rows: values.astype(jnp.float32) + offset_rows[2], inputs, offsets
    )
    summed = lax.psum((partials[0], partials[1]), "mp")
    normed = each_stream(
        lambda base_rows, extra_rows, gain_row, offset_rows: normalize(
            base_rows + extra_rows, gain_row[0], offset_rows[0]
        ),
        bases,
        summed,
        gain_rows,
        offsets,
    )
    hidden = (normed[0][0], normed[1][0])
    units_first = (normed[0][1], normed[1][1])
    inverse_first = (normed[0][2], normed[1][2])
    up_weights = (text_up, layout_up)
    down_weights = (text_down, layout_down)
    hidden_low = tuple((values.astype(jnp.bfloat16) for values in hidden))
    pre_gelu = each_stream(
        lambda values, weight, bias_row: matmul(values, weight) + bias_row.astype(jnp.float32),
        hidden_low,
        up_weights,
        (text_up_bias, layout_up_bias),
    )
    activated = tuple(
        (jax.nn.gelu(values, approximate=False).astype(jnp.bfloat16) for values in pre_gelu)
    )
    down_parts = each_stream(matmul, activated, down_weights)
    residual_second = each_stream(
        lambda values, offset_rows: values + offset_rows[3], hidden, offsets
    )
    summed = lax.psum((down_parts[0], down_parts[1]), "mp")
    normed_second = each_stream(
        lambda base_rows, extra_rows, gain_row, offset_rows: normalize(
            base_rows + extra_rows, gain_row[1], offset_rows[1]
        ),
        residual_second,
        summed,
        gain_rows,
        offsets,
    )
    outputs = (normed_second[0][0], normed_second[1][0])
    cotangents = (text_cot.astype(jnp.float32), layout_cot.astype(jnp.float32))
    own_cot = tuple((own_rows(values) for values in cotangents))
    second_grad = each_stream(
        lambda cot_rows, normed_rows, gain_row: norm_back(
            cot_rows, normed_rows[1], normed_rows[2], gain_row[1]
        ),
        cotangents,
        normed_second,
        gain_rows,
    )
    second_own = tuple((own_rows(values) for values in second_grad))
    units_second = tuple((own_rows(normed_rows[1]) for normed_rows in normed_second))
    ffn_grads = each_stream(
        ffn_back, second_grad, activated, pre_gelu, hidden_low, up_weights, down_weights
    )
    summed = lax.psum((ffn_grads[0][3], ffn_grads[1][3]), "mp")
    hidden_grad = each_stream(
        lambda extra_rows, direct_rows: extra_rows + direct_rows, summed, second_grad
    )
    first_grad = each_stream(
        lambda gradient, gain_row, unit_rows, inverse: norm_back(
            gradient, unit_rows, inverse, gain_row[0]
        ),
        hidden_grad,
        gain_rows,
        units_first,
        inverse_first,
    )
    hidden_own = tuple((own_rows(values) for values in hidden_grad))
    first_own = tuple((own_rows(values) for values in first_grad))
    units_first_own = tuple((own_rows(values) for values in units_first))
    gain_grads = each_stream(
        lambda cot_rows, unit_second, hidden_rows, unit_first: jnp.stack(
            [jnp.sum(hidden_rows * unit_first, 0), jnp.sum(cot_rows * unit_second, 0)]
        ),
        own_cot,
        units_second,
        hidden_own,
        units_first_own,
    )
    offset_grads = each_stream(
        lambda cot_rows, hidden_rows, first_rows, second_rows: jnp.stack(
            [
                jnp.sum(hidden_rows, 0),
                jnp.sum(cot_rows, 0),
                jnp.sum(first_rows, 0),
                jnp.sum(second_rows, 0),
            ]
        ),
        own_cot,
        hidden_own,
        first_own,
        second_own,
    )
    out_grads = each_stream(out_back, first_grad, attended, out_weights)
    back_inputs = page_inputs + (log_total, paged(out_grads[0][1]), paged(out_grads[1][1]))
    text_pages, layout_pages = lax.map(page_backward, back_inputs)
    proj_grads = tuple(
        (
            jnp.moveaxis(values, 1, 0).reshape(3, row_count, -1)
            for values in (text_pages, layout_pages)
        )
    )
    proj_results = each_stream(proj_back, inputs, proj_grads, qkv_weights)
    summed = lax.psum((proj_results[0][2], proj_results[1][2]), "mp")
    input_full = each_stream(
        lambda extra_rows, direct_rows: extra_rows + direct_rows, summed, first_grad
    )
    input_grads = each_stream(
        lambda flag_rows, values: jnp.where(flag_rows, 0.0, values), flags, input_full
    )
    vector_grads = each_stream(
        lambda flag_rows, values: jnp.sum(jnp.where(flag_rows, values, 0.0), 0), flags, input_full
    )
    text_matrices = (
        lax.psum_scatter(proj_results[0][0], "dp", scatter_dimension=1, tiled=True),
        lax.psum_scatter(out_grads[0][0], "dp", scatter_dimension=1, tiled=True),
        lax.psum_scatter(ffn_grads[0][1], "dp", scatter_dimension=0, tiled=True),
        lax.psum_scatter(ffn_grads[0][0], "dp", scatter_dimension=1, tiled=True),
    )
    mixed = lax.psum(
        (
            proj_results[1][0],
            out_grads[1][0],
            ffn_grads[1][1],
            ffn_grads[1][0],
            proj_results[0][1],
            proj_results[1][1],
            ffn_grads[0][2],
            ffn_grads[1][2],
            vector_grads[0],
            vector_grads[1],
        ),
        "dp",
    )
    norms = lax.psum((gain_grads[0], offset_grads[0], gain_grads[1], offset_grads[1]), ("dp", "mp"))
    return (
        outputs[0],
        outputs[1],
        input_grads[0],
        input_grads[1],
        mixed[8],
        mixed[9],
        text_matrices[0],
        mixed[4],
        text_matrices[1],
        norms[1],
        norms[0],
        text_matrices[2],
        mixed[6],
        text_matrices[3],
        mixed[0],
        mixed[5],
        mixed[1],
        norms[3],
        norms[2],
        mixed[2],
        mixed[7],
        mixed[3],
    )


def solution(mesh):
    placed = (
        P("dp", None),
        P("dp", None),
        P("dp"),
        P("dp"),
        P("dp"),
        P(),
        P(),
        P(None, None, "mp"),
        P(None, "mp"),
        P("mp", None),
        P(),
        P(),
        P(None, "mp"),
        P("mp"),
        P("mp", None),
        P(None, None, "mp"),
        P(None, "mp"),
        P("mp", None),
        P(),
        P(),
        P(None, "mp"),
        P("mp"),
        P("mp", None),
        P("dp", None),
        P("dp", None),
    )
    return jax.shard_map(
        shards,
        mesh=mesh,
        in_specs=placed,
        out_specs=(
            P("dp", None),
            P("dp", None),
            P("dp", None),
            P("dp", None),
            P(),
            P(),
            P(None, "dp", "mp"),
            P(None, "mp"),
            P("mp", "dp"),
            P(),
            P(),
            P("dp", "mp"),
            P("mp"),
            P("mp", "dp"),
            P(None, None, "mp"),
            P(None, "mp"),
            P("mp", None),
            P(),
            P(),
            P(None, "mp"),
            P("mp"),
            P("mp", None),
        ),
        check_vma=False,
    )
```

profile of v0, /device:TPU:0, one launch (start us, length us, event | category | flops | bytes accessed | tf_op | source)
XLA Modules:
  0.0 1394.5 jit_solution(10339675343011586420)
XLA Ops:
  29.8 45.0 %while.26 = (s32[]{:T(128)}, bf16[3,512,384]{2,1,0:T(8,128)(2,1)}, bf16[3,512,96]{1,2,0:T(8,128)(2,1)}, f32[3,6,512]{2,1,0:T(8,128)}, bf16[3,512,384]{1,2,0:T(8,...) while((s32[]{:T(128)}, bf16[3,512,384]{2,1,0:T(8,128)(2,1)}, ...), condition=%wide.region_3.4_spmd, body=%wide.region_0.3_spmd.sunk | while | flops 519287808 | bytes 60267684 | solution.py:235
  86.2 144.2 %all-reduce.22.cloned.1.call-done = (f32[1536,768]{1,0:T(8,128)}, f32[1536,192]{0,1:T(8,128)}) async-done(((f32[1536,768]{1,0:T(8,128)}, f32[1536,192]{0,1:T(8,128)}), (f32[1536,768]{1,0:T(8,128)}, f32[1536,192]{0,1:T(8,128)})) %all-reduce.22.cloned.1.call-update) | async-done | bytes 5898256 | tf_op jit(solution)/shard_map/psum | solution.py:244
  253.0 25.1 %multiply_convert_fusion.8 = (bf16[1536,1536]{1,0:T(8,128)(2,1)S(1)}, f32[1536,1536]{1,0:T(8,128)}, f32[1536,1536]{1,0:T(8,128)}) fusion(f32[1536]{0:T(1024)S(1)} %copy-done.73, bf16[768,1536]{1,0:T(8,128)(2,1)S(1)} %copy-done, f32[1536,768]{1,0:T(8,128)S(1)} %subtract_multiply_fusion.4, f32[768]{0:T(1024)S(1)} %copy-done.65, f32[768]{0:T(1024)S(1)} %copy-done.52), kind=kOutput, calls=%fused_computation.66 | convolution fusion | flops 3783131136 | bytes 30683136 | tf_op jit(solution)/shard_map/dot_general | solution.py:180
  285.7 10.9 all-reduce.18.cloned.1.call-start
  296.6 134.3 %all-reduce.20.cloned.1.call-done = (f32[1536,768]{1,0:T(8,128)}, f32[1536,192]{0,1:T(8,128)}) async-done(((f32[1536,768]{1,0:T(8,128)}, f32[1536,192]{0,1:T(8,128)}), (f32[1536,768]{1,0:T(8,128)}, f32[1536,192]{0,1:T(8,128)})) %all-reduce.20.cloned.1.call-update) | async-done | bytes 5898256 | tf_op jit(solution)/shard_map/psum | solution.py:273
  448.5 12.8 convert_reduce_fusion
  473.7 140.5 %all-reduce.18.cloned.1.call-done = (f32[1536,768]{1,0:T(8,128)}, f32[1536,192]{0,1:T(8,128)}) async-done(((f32[1536,768]{1,0:T(8,128)}, f32[1536,192]{0,1:T(8,128)}), (f32[1536,768]{1,0:T(8,128)}, f32[1536,192]{0,1:T(8,128)})) %all-reduce.18.cloned.1.call-update) | async-done | bytes 5898256 | tf_op jit(solution)/shard_map/psum | solution.py:299
  629.4 237.0 %while.27 = (s32[]{:T(128)}, bf16[3,3,512,384]{3,2,0,1:T(8,128)(2,1)}, bf16[3,3,512,96]{2,3,1,0:T(8,128)(2,1)}, bf16[3,512,384]{1,2,0:T(8,128)(2,1)}, pred[3,512...) while((s32[]{:T(128)}, ...), condition=%wide.region_29.30_spmd, body=%wide.region_26.29_spmd.sunk | while | flops 1412105728 | bytes 146512608 | solution.py:340
  643.8 9.1 fusion.270
  652.9 10.0 fusion.271
  667.3 8.1 subtract_multiply_fusion.12
  679.3 12.1 fusion.267
  691.5 11.2 fusion.266
  722.6 9.1 fusion.270
  731.7 10.0 fusion.271
  746.1 8.1 subtract_multiply_fusion.12
  758.1 12.1 fusion.267
  770.2 11.2 fusion.266
  801.4 9.1 fusion.270
  810.5 10.0 fusion.271
  824.9 8.1 subtract_multiply_fusion.12
  836.9 12.1 fusion.267
  849.0 11.2 fusion.266
  892.6 9.9 fusion.77
  903.3 10.1 fusion.82
  934.6 40.2 %all-reduce.1 = (f32[4,768]{1,0:T(4,128)}, f32[2,768]{1,0:T(2,128)}, f32[4,192]{1,0:T(4,128)}, f32[2,192]{1,0:T(2,128)}) all-reduce(f32[4,768]{1,0:T(4,128)S(1)} %pad_maximum_fusion.1, f32[2,768]{1,0:T(2,128)S(1)} %pad_maximum_fusion.3, f32[4,192]{1,0:T(4,128)S(1)} %pad_maximum_fusion.4, ...), channel_id=1, replica_groups=mesh['dp'=16,'mp'=2] {'dp','mp'}, use_global_device_ids=true, to_apply=%region_44.45 | all-reduce | flops 5760 | bytes 46080 | tf_op jit(solution)/shard_map/psum | solution.py:379
  977.6 38.2 %all-reduce.14.cloned.1.call-done = (f32[3,768,384]{2,0,1:T(4,128)}, f32[3,192,96]{1,2,0:T(8,128)}, f32[96,192]{1,0:T(8,128)}, f32[192,384]{1,0:T(8,128)}, f32[384,192]{0,1:T(8,128)}) async-done(((f32[3,768,384]{2,0,1:T(4,128)}, f32[3,192,96]{1,2,0:T(8,128)}, f32[96,192]{1,0:T(8,128)}, f32[192,384]{1,0:T(8,128)}, f32[384,192]{0,1:T(8,128)}), (f32[3,768,384]{2,0,1:T(4,128)}, f32[3,192,96]{1,2,0:T(8,128)}, ...) | async-done | bytes 4423696
  1019.4 144.7 %all-reduce.16.cloned.1.call-done = (f32[1536,768]{1,0:T(8,128)}, f32[1536,192]{0,1:T(8,128)}) async-done(((f32[1536,768]{1,0:T(8,128)}, f32[1536,192]{0,1:T(8,128)}), (f32[1536,768]{1,0:T(8,128)}, f32[1536,192]{0,1:T(8,128)})) %all-reduce.16.cloned.1.call-update) | async-done | bytes 5898256 | tf_op jit(solution)/shard_map/psum | solution.py:348
  1172.4 62.3 %all-reduce.2 = (f32[768]{0:T(1024)}, f32[192]{0:T(256)}, f32[2,384]{1,0:T(2,128)}, f32[1536]{0:T(1024)}, f32[2,96]{1,0:T(2,128)}, /*index=5*/f32[384]{0:T(512)}) all-reduce(f32[768]{0:T(1024)S(1)} %get-tuple-element.409, f32[192]{0:T(256)S(1)} %get-tuple-element.416, ...), channel_id=1, replica_groups=mesh['dp'=16,'mp'=2] {'dp'}, use_global_device_ids=true, to_apply=%region_33.34 | all-reduce | flops 3840 | bytes 30720 | tf_op jit(solution)/shard_map/psum | solution.py:364
  1234.7 9.7 reduce-scatter.8.cloned.1.call-done
  1244.4 79.6 %reduce-scatter.6.cloned.1.call-done = f32[48,1536]{1,0:T(8,128)} async-done(((f32[768,1536]{1,0:T(8,128)}), f32[48,1536]{1,0:T(8,128)}) %reduce-scatter.6.cloned.1.call-update) | async-done | bytes 294928 | tf_op jit(solution)/shard_map/reduce_scatter | solution.py:361
  1324.0 61.3 %reduce-scatter.4.cloned.1.call-done = f32[384,48]{0,1:T(8,128)} async-done(((f32[384,768]{0,1:T(8,128)}), f32[384,48]{0,1:T(8,128)}) %reduce-scatter.4.cloned.1.call-update) | async-done | bytes 73744 | tf_op jit(solution)/shard_map/reduce_scatter | solution.py:360
  (466 shorter events, 301.7 us)
Async XLA Ops:
  7.2 245.7 %copy-start = (bf16[768,1536]{1,0:T(8,128)(2,1)S(1)}, bf16[768,1536]{1,0:T(8,128)(2,1)}, u32[]{:S(2)}) copy-start(bf16[768,1536]{1,0:T(8,128)(2,1)} %param.41) | copy-start | bytes 7077892
  7.2 223.2 %all-reduce.22.cloned.1.call-start = ((), (), s32[]{:S(2)}) async-start(), calls=%async_computation.10 | async-start | bytes 11796480 | tf_op jit(solution)/shard_map/psum | solution.py:244
  24.2 207.9 %copy-start.49 = (pred[1536]{0:T(1024)(128)(4,1)}, pred[1536]{0:T(1024)(128)(4,1)S(1)}, u32[]{:S(2)}) copy-start(pred[1536]{0:T(1024)(128)(4,1)S(1)} %broadcast_compare_fusion) | copy-start | bytes 4612
  81.1 149.3 %copy-start.20 = (bf16[1536,192]{0,1:T(8,128)(2,1)S(1)}, bf16[1536,192]{0,1:T(8,128)(2,1)}, u32[]{:S(2)}) copy-start(bf16[1536,192]{0,1:T(8,128)(2,1)} %param.30) | copy-start | bytes 1769476
  82.5 348.4 %all-reduce.20.cloned.1.call-start = ((), (), s32[]{:S(2)}) async-start(), calls=%async_computation.9 | async-start | bytes 11796480 | tf_op jit(solution)/shard_map/psum | solution.py:273
  86.2 147.6 %copy-start.64 = (f32[1,192]{1,0:T(1,128)}, f32[1,192]{1,0:T(1,128)S(1)}, u32[]{:S(2)}) copy-start(f32[1,192]{1,0:T(1,128)S(1)} %get-tuple-element.430) | copy-start | bytes 2308
  235.7 195.2 %copy-start.6 = (f32[1536,192]{0,1:T(8,128)}, f32[1536,192]{0,1:T(8,128)S(1)}, u32[]{:S(2)}) copy-start(f32[1536,192]{0,1:T(8,128)S(1)} %subtract_multiply_fusion.8) | copy-start | bytes 3538948
  243.1 9.9 copy-start.3
  243.1 9.8 copy-start.52
  243.1 9.8 copy-start.65
  243.2 9.8 copy-start.73
  252.9 27.4 %copy-start.88 = (bf16[1536,768]{1,0:T(8,128)(2,1)S(1)}, bf16[1536,768]{1,0:T(8,128)(2,1)}, u32[]{:S(2)}) copy-start(bf16[1536,768]{1,0:T(8,128)(2,1)} %param.43) | copy-start | bytes 7077892
  285.7 328.5 %all-reduce.18.cloned.1.call-start = ((), (), s32[]{:S(2)}) async-start(), calls=%async_computation.8 | async-start | bytes 11796480 | tf_op jit(solution)/shard_map/psum | solution.py:299
  435.6 33.5 %copy-start.18 = (f32[1536,192]{0,1:T(8,128)}, f32[1536,192]{0,1:T(8,128)S(1)}, u32[]{:S(2)}) copy-start(f32[1536,192]{0,1:T(8,128)S(1)} %get-tuple-element.418) | copy-start | bytes 3538948
  448.5 12.8 copy-start.11
  469.0 546.8 %all-reduce.14.cloned.1.call-start = ((), (), s32[]{:S(2)}) async-start(), calls=%async_computation.6 | async-start | bytes 11403264
  471.7 144.6 %copy-start.61 = (f32[1,192]{1,0:T(1,128)S(1)}, f32[1,192]{1,0:T(1,128)}, u32[]{:S(2)}) copy-start(f32[1,192]{1,0:T(1,128)} %get-tuple-element.434) | copy-start | bytes 2308
  471.7 146.2 %slice-start.2 = ((s8[4718592]{0:T(1024)(128)(4,1)}), s8[524288]{0:T(1024)(128)(4,1)S(1)}, s32[]{:S(2)}) async-start(s8[4718592]{0:T(1024)(128)(4,1)} %bitcast.268), calls=%async_computation.13 | async-start | bytes 1048576
  629.4 237.0 %copy-start.58 = (pred[1536]{0:T(1024)(128)(4,1)S(1)}, pred[1536]{0:T(1024)(128)(4,1)}, u32[]{:S(2)}) copy-start(pred[1536]{0:T(1024)(128)(4,1)} %copy-done.56) | copy-start | bytes 4612
  629.4 237.0 %copy-start.63 = (bf16[768]{0:T(1024)(128)(2,1)S(1)}, bf16[768]{0:T(1024)(128)(2,1)}, u32[]{:S(2)}) copy-start(bf16[768]{0:T(1024)(128)(2,1)} %param.34) | copy-start | bytes 4612
  629.8 45.7 %copy-start.22 = (bf16[3,512,384]{2,1,0:T(8,128)(2,1)}, bf16[3,512,384]{2,1,0:T(8,128)(2,1)S(1)}, u32[]{:S(2)}) copy-start(bf16[3,512,384]{2,1,0:T(8,128)(2,1)S(1)} %get-tuple-element.690) | copy-start | bytes 3538948 | tf_op jit(solution)/shard_map/while
  708.6 45.6 %copy-start.22 = (bf16[3,512,384]{2,1,0:T(8,128)(2,1)}, bf16[3,512,384]{2,1,0:T(8,128)(2,1)S(1)}, u32[]{:S(2)}) copy-start(bf16[3,512,384]{2,1,0:T(8,128)(2,1)S(1)} %get-tuple-element.690) | copy-start | bytes 3538948 | tf_op jit(solution)/shard_map/while
  787.4 45.6 %copy-start.22 = (bf16[3,512,384]{2,1,0:T(8,128)(2,1)}, bf16[3,512,384]{2,1,0:T(8,128)(2,1)S(1)}, u32[]{:S(2)}) copy-start(bf16[3,512,384]{2,1,0:T(8,128)(2,1)S(1)} %get-tuple-element.690) | copy-start | bytes 3538948 | tf_op jit(solution)/shard_map/while
  883.0 281.1 %all-reduce.16.cloned.1.call-start = ((), (), s32[]{:S(2)}) async-start(), calls=%async_computation.7 | async-start | bytes 11796480 | tf_op jit(solution)/shard_map/psum | solution.py:348
  892.6 351.9 %reduce-scatter.8.cloned.1.call-start = ((), (), s32[]{:S(2)}) async-start(), calls=%async_computation.5 | async-start | bytes 5013504 | tf_op jit(solution)/shard_map/reduce_scatter | solution.py:362
  902.6 421.4 %reduce-scatter.6.cloned.1.call-start = ((), (), s32[]{:S(2)}) async-start(), calls=%async_computation.4 | async-start | bytes 5013504 | tf_op jit(solution)/shard_map/reduce_scatter | solution.py:361
  913.4 471.9 %reduce-scatter.4.cloned.1.call-start = ((), (), s32[]{:S(2)}) async-start(), calls=%async_computation.3 | async-start | bytes 1253376 | tf_op jit(solution)/shard_map/reduce_scatter | solution.py:360
  919.5 10.5 slice-start.6
  1166.5 218.8 %copy-start.48 = (f32[96,192]{1,0:T(8,128)S(1)}, f32[96,192]{1,0:T(8,128)}, u32[]{:S(2)}) copy-start(f32[96,192]{1,0:T(8,128)} %get-tuple-element.711) | copy-start | bytes 221188
  1166.5 219.4 %copy-start.39 = (f32[192,384]{1,0:T(8,128)S(1)}, f32[192,384]{1,0:T(8,128)}, u32[]{:S(2)}) copy-start(f32[192,384]{1,0:T(8,128)} %get-tuple-element.714) | copy-start | bytes 884740
  1166.5 220.1 %copy-start.38 = (f32[384,192]{0,1:T(8,128)S(1)}, f32[384,192]{0,1:T(8,128)}, u32[]{:S(2)}) copy-start(f32[384,192]{0,1:T(8,128)} %get-tuple-element.716) | copy-start | bytes 884740
  1166.5 220.8 %copy-start.1 = (bf16[768,1536]{1,0:T(8,128)(2,1)S(1)}, bf16[768,1536]{1,0:T(8,128)(2,1)}, u32[]{:S(2)}) copy-start(bf16[768,1536]{1,0:T(8,128)(2,1)} %param.41) | copy-start | bytes 7077892
  (87 other events, 315.7 us)
Sparse Core Ops, SparseCore 0:
  82.6 147.7 all-reduce.21
  285.8 145.0 all-reduce.19
  469.1 145.0 all-reduce.17
  883.1 132.6 all-reduce.13
  1018.9 145.1 all-reduce.15
  1168.4 76.0 reduce-scatter.7
  1249.4 74.5 reduce-scatter.5
  1328.2 57.0 reduce-scatter.3
where the time goes:
time: 1400 us; the launch traced here: 1390 us
  waiting for transfers between devices  753 us (54%)
  matrix products  351 us (25%)
  blocking collectives  103 us (7%)
  local copies, waits for them, and re-layouts  89.7 us (6%)
  other arithmetic  70.1 us (5%)
  between operations  16.4 us (1%)
    psum x1, waiting for transfers between devices, shards(): summed = lax.psum((proj_results[0][2], proj_results[1][2]), 'mp')  145 us
    psum x1, waiting for transfers between devices, shards(): summed = lax.psum((partials[0], partials[1]), 'mp')  144 us
    psum x1, waiting for transfers between devices, shards(): summed = lax.psum((ffn_grads[0][3], ffn_grads[1][3]), 'mp')  141 us
    psum x1, waiting for transfers between devices, shards(): summed = lax.psum((down_parts[0], down_parts[1]), 'mp')  134 us
    reduce_scatter x1, waiting for transfers between devices, shards(): lax.psum_scatter(ffn_grads[0][1], 'dp', scatter_dimension=0, tiled=True)  79.6 us
    dot_general x6, matrix products, input_grads(): jnp.einsum('hqk,khd->qhd', score_round, split_heads(keys_in, head_width),...  66.3 us
    psum x1, blocking collectives, shards(): lax.psum((proj_results[1][0], out_grads[1][0], ffn_grads[1][1], ffn_grads...  62.3 us
    reduce_scatter x1, waiting for transfers between devices, shards(): lax.psum_scatter(out_grads[0][0], 'dp', scatter_dimension=1, tiled=True)  61.3 us
  transfers between devices with their start and end apart: 8, of which 8 were waited for; matrix products, arithmetic and copies ran while one was open for 5% of the time, Pallas kernels for 0%

commit v1 on v0

v1 whole, which is shorter than its diff:
```python
import functools
import jax, jax.numpy as jnp
from jax import lax
from jax.experimental import pallas as pl
from jax.experimental.pallas import tpu as pltpu
F32=jnp.float32; BF=jnp.bfloat16
NT=(((1,),(1,)),((),()))
TN=(((0,),(0,)),((),()))
def dot(a,b): return jnp.dot(a,b,preferred_element_type=F32)
def dotg(a,b,dn): return lax.dot_general(a,b,dn,preferred_element_type=F32)
VLIM=60*1024*1024

def lane_iota(shape): return lax.broadcasted_iota(jnp.int32,shape,len(shape)-1)

def attn_fwd_kernel(len_ref, xt_ref, xl_ref, wt_ref, wl_ref, bt_ref, bl_ref,
                    qt_ref, kt_ref, vt_ref, ql_ref, kl_ref, vl_ref, ot_ref, ol_ref, lse_ref, olT, lseT):
    page=pl.program_id(0)
    seq=xt_ref.shape[0]
    xt=xt_ref[...]; xl=xl_ref[...]
    for c,(t,l) in enumerate(((qt_ref,ql_ref),(kt_ref,kl_ref),(vt_ref,vl_ref))):
        t[...]=(dot(xt,wt_ref[c])+bt_ref[c:c+1,:]).astype(BF)
        l[...]=(dot(xl,wl_ref[c])+bl_ref[c:c+1,:]).astype(BF)
    lane=lane_iota((seq,128))
    row=lax.broadcasted_iota(jnp.int32,(seq,128),0)
    length=len_ref[page]
    bias=jnp.where(row<length,0.0,-1e9).astype(BF)
    one=jnp.ones((seq,128),BF)
    ql=jnp.where(lane==96,one,ql_ref[...]*BF(0.25))
    kl=jnp.where(lane==96,bias,kl_ref[...])
    vlT=vl_ref[...].T
    zero=jnp.zeros((seq,128),BF)
    olT[...]=jnp.zeros_like(olT); lseT[...]=jnp.zeros_like(lseT)
    for j in range(3):
        cols=slice(128*j,128*j+128)
        qbig=jnp.concatenate([qt_ref[:,cols]*BF(0.125),ql],1)
        vT=vt_ref[:,cols].T
        halves=[]
        for s in range(2):
            h=2*j+s
            kbig=jnp.concatenate([jnp.where(lane//64==s,kt_ref[:,cols],zero),
                                  jnp.where((lane//16==h)|(lane==96),kl,zero)],1)
            S=dotg(kbig,qbig,NT)
            m=jnp.max(S,0,keepdims=True)
            e=jnp.exp(S-m)
            ssum=jnp.sum(e,0,keepdims=True)
            v80=jnp.concatenate([vT[64*s:64*s+64],vlT[16*h:16*h+16]],0)
            o=dot(v80,e.astype(BF))*(1.0/ssum)
            halves.append(o[:64])
            olT[16*h:16*h+16,:]=o[64:]
            lseT[h:h+1,:]=m+jnp.log(ssum)
        ot_ref[:,cols]=jnp.concatenate(halves,0).T.astype(BF)
    ol_ref[...]=olT[...].T.astype(BF)
    lse_ref[...]=pltpu.roll(lseT[...].T,97,1)

def attn_fwd(lengths, xt, xl, wt, wl, bt, bl):
    rows=xt.shape[0]; pages=lengths.shape[0]; seq=rows//pages
    rb=lambda n: pl.BlockSpec((seq,n),lambda p,*_:(p,0))
    full=lambda a: pl.BlockSpec(a.shape,lambda p,*_:(0,)*a.ndim)
    o=lambda n,d=BF: jax.ShapeDtypeStruct((rows,n),d)
    return pl.pallas_call(attn_fwd_kernel,
        grid_spec=pltpu.PrefetchScalarGridSpec(num_scalar_prefetch=1,grid=(pages,),
            in_specs=[rb(768),rb(192),full(wt),full(wl),full(bt),full(bl)],
            out_specs=[rb(384)]*3+[rb(128)]*3+[rb(384),rb(128),rb(128)],
            scratch_shapes=[pltpu.VMEM((128,seq),F32),pltpu.VMEM((128,seq),F32)]),
        out_shape=[o(384)]*3+[o(128)]*3+[o(384),o(128),o(128,F32)],
        compiler_params=pltpu.CompilerParams(vmem_limit_bytes=VLIM),name="attn_fwd")(lengths,xt,xl,wt,wl,bt,bl)

def ind_matrix(j):
    r=lax.broadcasted_iota(jnp.int32,(256,128),0)%128
    l=lax.broadcasted_iota(jnp.int32,(256,128),1)
    h=(r//64+2*j) if j is not None else r//16
    return jnp.where((l==97+h)&(h<6),1.0,0.0).astype(BF)

def split2(v):
    hi=v.astype(BF)
    return hi,(v-hi.astype(F32)).astype(BF)

def attn_bwd_kernel(mode, len_ref, qt_ref, kt_ref, vt_ref, ql_ref, kl_ref, vl_ref, ot_ref, ol_ref, lse_ref, dot_ref, dol_ref,
                    dpt_ref, dpl_ref, dqlT):
    page=pl.program_id(0)
    seq=qt_ref.shape[0]
    lane=lane_iota((seq,128))
    row=lax.broadcasted_iota(jnp.int32,(seq,128),0)
    bias=jnp.where(row<len_ref[page],0.0,-1e9).astype(BF)
    zero=jnp.zeros((seq,128),BF); one=jnp.ones((seq,128),BF)
    nl=-lse_ref[...]
    hi=nl.astype(BF); r1=nl-hi.astype(F32); mid=r1.astype(BF); lo=r1-mid.astype(F32)
    ext=hi+pltpu.roll(mid.astype(F32),7,1).astype(BF)+pltpu.roll(lo,14,1).astype(BF)
    qle=jnp.where(lane<96,ql_ref[...]*BF(0.25),jnp.where(lane==96,one,ext))
    kl=kl_ref[...]; vl=vl_ref[...]; ql=ql_ref[...]
    if mode==2:
        klT=kl.T
        dqlT[...]=jnp.zeros_like(dqlT)
    def sums(a,b,m):
        p=a.astype(F32)*b.astype(F32)
        h_,l_=split2(p)
        return dot(jnp.concatenate([h_,l_],1),m)
    dol=dol_ref[...]
    d_l=sums(dol,ol_ref[...],ind_matrix(None))
    d_t=d_l
    for j in range(3):
        cols=slice(128*j,128*j+128)
        d_t=d_t+sums(dot_ref[:,cols],ot_ref[:,cols],ind_matrix(j))
    def ext_delta(d):
        h_=d.astype(BF); l_=d-h_.astype(F32)
        return h_+pltpu.roll(l_,7,1).astype(BF)
    dol1=jnp.where(lane<96,dol*BF(0.125),ext_delta(d_t*-0.125))
    dol2=jnp.where(lane<96,dol*BF(0.25),ext_delta(d_l*-0.25))
    for j in range(3):
        cols=slice(128*j,128*j+128)
        qt=qt_ref[:,cols]; kt=kt_ref[:,cols]; vt=vt_ref[:,cols]; dO=dot_ref[:,cols]
        qbig=jnp.concatenate([qt*BF(0.125),qle],1)
        dbig=jnp.concatenate([dO*BF(0.125),dol1],1)
        dObig=jnp.concatenate([dO,dol],1)
        prev=None
        if mode==2: ktT=kt.T
        for s in range(2):
            h=2*j+s
            tm=lane//64==s; lm=lane//16==h
            kbig=jnp.concatenate([jnp.where(tm,kt,zero),jnp.where(lm,kl,jnp.where(lane==96,bias,
                 jnp.where((lane==97+h)|(lane==104+h)|(lane==111+h),one,zero)))],1)
            vle=jnp.where(lm,vl,jnp.where((lane==97+h)|(lane==104+h),one,zero))
            vbig=jnp.concatenate([jnp.where(tm,vt,zero),vle],1)
            S=dotg(kbig,qbig,NT)
            M1=dotg(vbig,dbig,NT)
            M2=dotg(vle,dol2,NT)
            Pm=jnp.exp(S)
            Pb=Pm.astype(BF)
            R1=(Pm*M1).astype(BF)
            R2=(Pm*M2).astype(BF)
            dk_t=dot(R1,qt); dk_l=dot(R2,ql); dv=dot(Pb,dObig)
            if mode==0:
                dq_t=dotg(R1,kt,TN); dq_l=dotg(R2,kl,TN)
            elif mode==2:
                dq_t=dot(ktT[64*s:64*s+64],R1)
                dq_l=dot(klT[16*h:16*h+16],R2)
            elif mode==1:
                dq_t=dotg(kt,R1,TN).T; dq_l=dotg(kl,R2,TN).T
            cur=(dq_t,dk_t,dv[:,:128])
            curl=(dq_l,dk_l,dv[:,128:])
            if mode==2:
                dqlT[16*h:16*h+16,:]=dq_l
                if s==1:
                    dpt_ref[0,:,cols]=jnp.concatenate([prev[0],dq_t],0).T.astype(BF)
            for c in range(1 if mode==2 else 0,3):
                if s==1:
                    dpt_ref[c,:,cols]=jnp.where(lane<64,prev[c],cur[c]).astype(BF)
                pv=jnp.zeros((seq,128),BF) if h==0 else dpl_ref[c]
                dpl_ref[c]=jnp.where(lm,curl[c].astype(BF),pv)
            prev=cur
    if mode==2: dpl_ref[0]=dqlT[...].T.astype(BF)

def attn_bwd(mode,lengths,qt,kt,vt,ql,kl,vl,ot,ol,lse,dO,dol):
    rows=qt.shape[0]; pages=lengths.shape[0]; seq=rows//pages
    rb=lambda n: pl.BlockSpec((seq,n),lambda p,*_:(p,0))
    return pl.pallas_call(functools.partial(attn_bwd_kernel,mode),
        grid_spec=pltpu.PrefetchScalarGridSpec(num_scalar_prefetch=1,grid=(pages,),
            in_specs=[rb(384)]*3+[rb(128)]*3+[rb(384),rb(128),rb(128),rb(384),rb(128)],
            out_specs=[pl.BlockSpec((3,seq,384),lambda p,*_:(0,p,0)),pl.BlockSpec((3,seq,128),lambda p,*_:(0,p,0))],
            scratch_shapes=[pltpu.VMEM((128,seq),F32)]),
        out_shape=[jax.ShapeDtypeStruct((3,rows,384),BF),jax.ShapeDtypeStruct((3,rows,128),BF)],
        compiler_params=pltpu.CompilerParams(vmem_limit_bytes=VLIM),name=f"attn_bwd{mode}")(lengths,qt,kt,vt,ql,kl,vl,ot,ol,lse,dO,dol)


EPS=1e-5
def gelu_parts(x):
    cdf=0.5+0.5*lax.erf(x*0.7071067811865476)
    phi=jnp.exp2(x*x*-0.7213475204444817-1.3257480647361593)
    return cdf, cdf+x*phi

def norm(v):
    mu=jnp.mean(v,-1,keepdims=True)
    c=v-mu
    inv=lax.rsqrt(jnp.mean(c*c,-1,keepdims=True)+EPS)
    return c*inv,inv

def norm_back(g,u,inv,gain):
    s=g*gain
    return inv*(s-jnp.mean(s,-1,keepdims=True)-u*jnp.mean(s*u,-1,keepdims=True))

def stream(own_col, own_off, x, o, o_own, cot, outw, up, down, shift, gain, upb, act, gp, out_ref, dr1_ref, dos, gup, gdn, gout, stat, bstat, first, chunk):
    d=x.shape[1]; F=up.shape[1]; half=F//2
    h1u,i1=norm(x.astype(F32)+dot(o,outw[...])+shift[2:3])
    h1=h1u*gain[0:1]+shift[0:1]
    h1b=h1.astype(BF)
    for f in range(0,F,chunk):
        cs=slice(f,f+chunk)
        pre=dot(h1b,up[:,cs])+upb[:,cs]
        cdf,der=gelu_parts(pre)
        act[:,cs]=(pre*cdf).astype(BF)
        gp[:,cs]=der.astype(BF)
    r2=h1+dot(act[...],down[...])+shift[3:4]
    u2,i2=norm(r2)
    out_ref[...]=u2*gain[1:2]+shift[1:2]
    g=cot.astype(F32)
    dr2=norm_back(g,u2,i2,gain[1:2])
    dr2b=dr2.astype(BF)
    for f in range(0,F,chunk):
        cs=slice(f,f+chunk)
        da=dotg(dr2b,down[cs,:],NT)
        gp[:,cs]=(da*gp[:,cs].astype(F32)).astype(BF)
    dh1=dotg(gp[...],up[...],NT)+dr2
    dr1=norm_back(dh1,h1u,i1,gain[0:1])
    dr1_ref[...]=dr1
    dr1b=dr1.astype(BF)
    dO=dotg(dr1b,outw[...],NT).astype(BF)
    w=dO.shape[1]//2
    dos[0]=dO[:,:w]; dos[1]=dO[:,w:]
    osl=pl.ds(pl.multiple_of(own_off,128),half)
    dpo=gp[:,osl]
    ones=jnp.ones((8,x.shape[0]),BF)
    rs=lambda v: jnp.sum(v,0,keepdims=True)
    st=jnp.concatenate([rs(dh1),rs(g),rs(dr1),rs(dr2),rs(dh1*h1u),rs(g*u2),jnp.zeros((2,d),F32)],0)
    def put(first):
        for ref,a,b in ((gup,h1b,dpo),(gdn,dr2b,act[:,osl]),(gout,dr1b,o_own)):
            v=dotg(a,b,TN)
            if first: ref[...]=v
            else: ref[...]+=v
        b=dot(ones,dpo)
        if first:
            stat[...]=st; bstat[...]=b
        else:
            stat[...]+=st; bstat[...]+=b
    pl.when(first)(lambda: put(True))
    pl.when(jnp.logical_not(first))(lambda: put(False))

def ffn_kernel(mp_ref, xt, xl, oa, ob, ola, olb, ct, cl, outw, up, down, sh, ga, upb, outwl, upl, downl, shl, gal, upbl,
               to, lo, dr1, dr1l, dos, dosl, gup, gdn, gout, st, bst, gupl, gdnl, goutl, stl, bstl, act, gp, actl, gpl):
    mp=mp_ref[0]
    first=pl.program_id(0)==0
    def both(a,b):
        a=a[...]; b=b[...]
        z=mp==0
        return jnp.concatenate([jnp.where(z,a,b),jnp.where(z,b,a)],1)
    stream(None,mp*1536,xt[...],both(oa,ob),oa[...],ct[...],outw,up,down,sh,ga,upb,act,gp,to,dr1,dos,gup,gdn,gout,st,bst,first,512)
    stream(None,mp*384,xl[...],both(ola,olb),ola[...],cl[...],outwl,upl,downl,shl,gal,upbl,actl,gpl,lo,dr1l,dosl,gupl,gdnl,goutl,stl,bstl,first,768)

def ffn(mp,xt,xl,oa,ob,ola,olb,ct,cl,wts,tile=384):
    rows=xt.shape[0]
    rb=lambda a: pl.BlockSpec((tile,a.shape[1]),lambda p,*_:(p,0))
    full=lambda a: pl.BlockSpec(a.shape,lambda p,*_:(0,)*len(a.shape),pipeline_mode=pl.Buffered(1))
    S=jax.ShapeDtypeStruct
    ins=[xt,xl,oa,ob,ola,olb,ct,cl]
    rowout=[S((rows,768),F32),S((rows,192),F32),S((rows,768),F32),S((rows,192),F32)]
    dos=[S((2,rows,384),BF),S((2,rows,128),BF)]
    acc=[S((768,1536),F32),S((768,1536),F32),S((768,384),F32),S((8,768),F32),S((8,1536),F32),
         S((192,384),F32),S((192,384),F32),S((192,128),F32),S((8,192),F32),S((8,384),F32)]
    return pl.pallas_call(ffn_kernel,
        grid_spec=pltpu.PrefetchScalarGridSpec(num_scalar_prefetch=1,grid=(rows//tile,),
            in_specs=[rb(a) for a in ins]+[full(w) for w in wts],
            out_specs=[rb(a) for a in rowout]+[pl.BlockSpec((2,tile,a.shape[2]),lambda p,*_:(0,p,0)) for a in dos]+[full(a) for a in acc],
            scratch_shapes=[pltpu.VMEM((tile,3072),BF),pltpu.VMEM((tile,3072),BF),pltpu.VMEM((tile,768),BF),pltpu.VMEM((tile,768),BF)]),
        out_shape=rowout+dos+acc,
        compiler_params=pltpu.CompilerParams(vmem_limit_bytes=VLIM),name="middle")(mp,*ins,*wts)


from jax.sharding import PartitionSpec as P


def pack_kernel(idx_ref, *refs):
    out=refs[-1]
    out[...]=jnp.zeros_like(out)
    r=0
    for src in refs[:-1]:
        lead=src.shape[0] if len(src.shape)==3 else None
        for c in range(lead or 1):
            w=src[c] if lead else src[...]
            n,m=w.shape
            for j in range(0,m,128):
                e=min(128,m-j)
                out[r:r+n,:e]=w[:,j:j+e].astype(F32)
                r+=n


def pack(idx, split, whole, parts):
    specs=[]; n=0
    for a in split:
        rows=a.shape[-2]//parts
        blocks=-(-a.shape[-1]//128)
        if a.ndim==3:
            specs.append(pl.BlockSpec((a.shape[0],rows,a.shape[2]),lambda i,s:(0,s[0],0)))
            n+=a.shape[0]*rows*blocks
        else:
            specs.append(pl.BlockSpec((rows,a.shape[1]),lambda i,s:(s[0],0)))
            n+=rows*blocks
    for a in whole:
        specs.append(pl.BlockSpec(a.shape,lambda i,s:(0,0)))
        n+=a.shape[0]*(-(-a.shape[1]//128))
    n=-(-n//8)*8
    return pl.pallas_call(pack_kernel,
        grid_spec=pltpu.PrefetchScalarGridSpec(num_scalar_prefetch=1,grid=(1,),in_specs=specs,
            out_specs=pl.BlockSpec((n,128),lambda i,s:(0,0))),
        out_shape=jax.ShapeDtypeStruct((n,128),F32),
        compiler_params=pltpu.CompilerParams(vmem_limit_bytes=VLIM),name="pack")(idx,*split,*whole)


def unpack_first_kernel(s_ref, pa, pb, pc, pd, o_own, u_own, d_own, wt, wl, bt, bl, outl, upl, downl, upb, upbl, s48, s24, s96, su):
    mp=s_ref[0]; other=1-mp
    wl[...]=jnp.zeros_like(wl); outl[...]=jnp.zeros_like(outl); s24[...]=jnp.zeros_like(s24)
    bt[...]=jnp.zeros_like(bt); bl[...]=jnp.zeros_like(bl)
    for p,ref in enumerate((pa,pb,pc,pd)):
        i=s_ref[1+p]
        at=lambda n: pl.ds(pl.multiple_of(i*n,n),n)
        r=0
        for c in range(3):
            for j in range(3):
                wt[c,at(192),128*j:128*j+128]=ref[r:r+192].astype(BF); r+=192
        for c in range(3):
            wl[c,at(48),:]=ref[r:r+48].astype(BF); r+=48
        s24[at(24),:128]=ref[r:r+24]; r+=24
        s24[at(24),128:]=ref[r:r+24,:64]; r+=24
        for j in range(3):
            su[at(48),128*j:128*j+128]=ref[r:r+48].astype(BF); r+=48
        s96[at(96),:128]=ref[r:r+96].astype(BF); r+=96
        s96[at(96),128:]=ref[r:r+96,:64].astype(BF); r+=96
        if p==0:
            for c in range(2):
                for j in range(3):
                    bt[2*c:2*c+1,128*j:128*j+128]=ref[r+2*j+c:r+2*j+c+1]
            r+=6
            for c in range(2):
                bl[2*c:2*c+1,:]=ref[r+c:r+c+1]
            r+=2
            base=pl.multiple_of(other*1536,128)
            for j in range(12):
                upb[:,pl.ds(base+128*j,128)]=ref[r+j:r+j+1]
            r+=12
            base=pl.multiple_of(other*384,128)
            for j in range(3):
                upbl[:,pl.ds(base+128*j,128)]=ref[r+j:r+j+1]
    half=lambda k,n: pl.ds(pl.multiple_of(k*n,n),n)
    outl[half(mp,128),:]=jnp.concatenate([o_own[...],jnp.zeros((32,192),BF)],0)
    outl[half(other,128),:]=s24[...].astype(BF)
    upl[:,half(mp,384)]=u_own[...]; upl[:,half(other,384)]=su[...]
    downl[half(mp,384),:]=d_own[...]; downl[half(other,384),:]=s96[...]


def unpack_first(scal, pieces, o_own, u_own, d_own, ub_own, ubl_own):
    S=jax.ShapeDtypeStruct
    full=lambda a: pl.BlockSpec(a.shape,lambda i,*_:(0,)*len(a.shape))
    outs=[S((3,768,384),BF),S((3,192,128),BF),S((3,384),F32),S((3,128),F32),S((256,192),BF),S((192,768),BF),S((768,192),BF),S((1,3072),F32),S((1,768),F32)]
    ins=[*pieces,o_own,u_own,d_own]
    res=pl.pallas_call(unpack_first_kernel,
        grid_spec=pltpu.PrefetchScalarGridSpec(num_scalar_prefetch=1,grid=(1,),in_specs=[full(a) for a in ins],
            out_specs=[full(a) for a in outs],
            scratch_shapes=[pltpu.VMEM((8,128),F32),pltpu.VMEM((128,192),F32),pltpu.VMEM((384,192),BF),pltpu.VMEM((192,384),BF)]),
        out_shape=outs,compiler_params=pltpu.CompilerParams(vmem_limit_bytes=VLIM),name="unpack_first")(scal,*ins)
    return res


def unpack_rows_kernel(parts, axis, s_ref, *refs):
    pieces=refs[:parts]; own=refs[parts]; out=refs[parts+1]
    mp=s_ref[0]; other=1-mp
    n,m=own.shape
    rows=n//parts
    if axis==1:
        out[:,pl.ds(pl.multiple_of(mp*m,128),m)]=own[...]
    else:
        out[pl.ds(pl.multiple_of(mp*n,n),n),:]=own[...]
    for p,ref in enumerate(pieces):
        i=s_ref[1+p]
        for j in range(m//128):
            v=ref[j*rows:j*rows+rows].astype(BF)
            if axis==1:
                out[pl.ds(pl.multiple_of(i*rows,rows),rows),pl.ds(pl.multiple_of(other*m+128*j,128),128)]=v
            else:
                out[pl.ds(pl.multiple_of(other*n+i*rows,rows),rows),128*j:128*j+128]=v


def unpack_rows(scal, pieces, own, axis, offset=0):
    parts=len(pieces)
    n,m=own.shape
    rows=n//parts*(m//128)
    shape=(n,2*m) if axis==1 else (2*n,m)
    return pl.pallas_call(functools.partial(unpack_rows_kernel,parts,axis),
        grid_spec=pltpu.PrefetchScalarGridSpec(num_scalar_prefetch=1,grid=(1,),
            in_specs=[pl.BlockSpec((rows,128),lambda i,*_:(offset,0)) for _ in pieces]+[pl.BlockSpec(own.shape,lambda i,*_:(0,0))],
            out_specs=pl.BlockSpec(shape,lambda i,*_:(0,0))),
        out_shape=jax.ShapeDtypeStruct(shape,BF),
        compiler_params=pltpu.CompilerParams(vmem_limit_bytes=VLIM),name="unpack")(scal,*pieces,own)


def flip(n, bit):
    return [(i,i^bit) for i in range(n)]


def cross(n):
    return [(i,i^(2 if i%2==0 else 4)) for i in range(n)]


def gather_pieces(piece, n):
    a=lax.ppermute(piece,"mp",[(0,1),(1,0)])
    b=lax.ppermute(a,"dp",cross(n))
    c=lax.ppermute(a,"dp",flip(n,1))
    d=lax.ppermute(b,"dp",flip(n,1))
    return a,b,c,d


def bias_rows(pair):
    b=pair.astype(F32)
    return jnp.stack([b[0],jnp.zeros_like(b[0]),b[1]])


def shards(text_in, layout_in, token_mask, box_mask, lengths, text_mask_vec, layout_mask_vec,
           text_qkv, text_qv_bias, text_out_w, text_shifts, text_gains, text_up, text_up_bias, text_down,
           layout_qkv, layout_qv_bias, layout_out_w, layout_shifts, layout_gains, layout_up, layout_up_bias, layout_down,
           text_cot, layout_cot):
    n=lax.axis_size("dp")
    mp=lax.axis_index("mp").astype(jnp.int32); dp=lax.axis_index("dp").astype(jnp.int32)
    core=dp&1; color=((dp>>1)^(dp>>2))&1
    ids=[2*color+core,2*(1-color)+core,2*color+1-core,2*(1-color)+1-core]
    scal=jnp.stack([mp]+ids)
    idx=ids[0][None]
    first=gather_pieces(pack(idx,[text_qkv,layout_qkv,layout_out_w,layout_up,layout_down],
        [text_qv_bias,layout_qv_bias,text_up_bias[None],layout_up_bias[None]],4),n)
    outp=gather_pieces(pack(idx,[text_out_w],[],4),n)
    upp=gather_pieces(pack(idx,[text_up],[],4),n)
    downp=gather_pieces(pack(idx,[text_down],[],4),n)

    tflag=token_mask[:,None]==1; lflag=box_mask[:,None]==1
    xt=jnp.where(tflag,text_mask_vec[None],text_in)
    xl=jnp.where(lflag,layout_mask_vec[None],layout_in)
    pad=lambda v: jnp.pad(v,((0,0),)*(v.ndim-1)+((0,32),))
    own=attn_fwd(lengths,xt,xl,text_qkv,pad(layout_qkv),bias_rows(text_qv_bias),pad(bias_rows(layout_qv_bias)))
    wt_o,wl_o,bt_o,bl_o,outl,upl,downl,upb,upbl=unpack_first(scal,first,layout_out_w,layout_up,layout_down,None,None)
    place=lambda full,half: lax.dynamic_update_slice(full,half.astype(F32)[None],(0,mp*half.shape[0]))
    upb=place(upb,text_up_bias); upbl=place(upbl,layout_up_bias)
    oth=attn_fwd(lengths,xt,xl,wt_o,wl_o,bt_o,bl_o)
    outw=unpack_rows(scal,outp,text_out_w,0)
    up=unpack_rows(scal,upp,text_up,1)
    down=unpack_rows(scal,downp,text_down,0)
    ws=[outw,up,down,text_shifts.astype(F32),text_gains.astype(F32),upb,outl,upl,downl,layout_shifts.astype(F32),layout_gains.astype(F32),upbl]
    (to,lo,dr1,dr1l,dO,dOl,gup,gdn,gout,st,bst,gupl,gdnl,goutl,stl,bstl)=ffn(mp[None],xt,xl,own[6],oth[6],own[7],oth[7],text_cot,layout_cot,ws)
    rs=lambda v: lax.psum_scatter(v,"dp",scatter_dimension=v.ndim-2,tiled=True)
    gup=rs(gup); gdn=rs(gdn); gout=rs(gout)
    pick=lambda v,k: lax.dynamic_index_in_dim(v,k,0,keepdims=False)
    d_own=attn_bwd(2,lengths,*own,pick(dO,mp),pick(dOl,mp))
    qg=jnp.einsum("nd,cne->cde",xt,d_own[0],preferred_element_type=F32)
    qgl=jnp.einsum("nd,cne->cde",xl,d_own[1],preferred_element_type=F32)[:,:,:96]
    cs=jnp.sum(d_own[0],1,dtype=F32); csl=jnp.sum(d_own[1],1,dtype=F32)[:,:96]
    qg=rs(qg)
    d_oth=attn_bwd(2,lengths,*oth,pick(dO,1-mp),pick(dOl,1-mp))
    back=lambda d,w: jnp.einsum("cne,cde->nd",d,w,preferred_element_type=F32)
    ta=back(d_own[0],text_qkv); tb=back(d_oth[0],wt_o)
    la=back(d_own[1],pad(layout_qkv)); lb=back(d_oth[1],wl_o)
    dx=(ta+tb)+dr1; dxl=(la+lb)+dr1l
    tg=jnp.where(tflag,0.0,dx); lg=jnp.where(lflag,0.0,dxl)
    tv=jnp.sum(jnp.where(tflag,dx,0.0),0); lv=jnp.sum(jnp.where(lflag,dxl,0.0),0)
    mixed=lax.psum((qgl,goutl[:,:96].T,gupl,gdnl.T,cs[0::2],csl[0::2],bst[0],bstl[0],tv,lv,st[:6],stl[:6]),"dp")
    qgl,goutl,gupl,gdnl,cs,csl,bst,bstl,tv,lv,st,stl=mixed
    return (to,lo,tg,lg,tv,lv,qg,cs,gout.T,st[:4],st[4:],gup,bst,gdn.T,
            qgl,csl,goutl,stl[:4],stl[4:],gupl,bstl,gdnl)


def solution(mesh):
    rows=P("dp",None); cols=P(None,"mp"); lead=P("mp",None); cube=P(None,None,"mp")
    weights=(cube,cols,lead,P(),P(),cols,P("mp"),lead)
    return jax.shard_map(shards,mesh=mesh,
        in_specs=(rows,rows,P("dp"),P("dp"),P("dp"),P(),P())+weights+weights+(rows,rows),
        out_specs=(rows,rows,rows,rows,P(),P(),P(None,"dp","mp"),cols,P("mp","dp"),P(),P(),P("dp","mp"),P("mp"),P("mp","dp"),
                   cube,cols,lead,P(),P(),cols,P("mp"),lead),
        check_vma=False)
```

time: 1400 us -> 703 us (0.50)
  waiting for transfers between devices: 753 us -> 349 us
  matrix products: 351 us -> 16.7 us
  Pallas kernels: 0 us -> 199 us
  other arithmetic: 70.1 us -> 11.6 us
  local copies, waits for them, and re-layouts: 89.7 us -> 33.4 us
  blocking collectives: 103 us -> 63.9 us
    psum x4 -> x0, waiting for transfers between devices: 564 us -> none  [the longest x1 145 us: shards(): summed = lax.psum((proj_results[0][2], proj_results[1][2]), 'mp')]
    dot_general x65 -> x6, matrix products: 326 us -> 16.7 us  [the longest x4 8.67 us: shards(): jnp.einsum('cne,cde->nd', d, w, preferred_element_type=F32)]
    pallas_call x0 -> x13, Pallas kernels: none -> 199 us  [the longest x1 83.7 us: ffn(): pl.pallas_call(ffn_kernel, grid_spec=pltpu.PrefetchScalarGridSpec(num_sca...]
    ppermute x0 -> x16, waiting for transfers between devices: none -> 110 us  [the longest x4 72.8 us: gather_pieces(): a = lax.ppermute(piece, 'mp', [(0, 1), (1, 0)])]
    reduce_scatter x3, waiting for transfers between devices: 151 us -> 217 us  [shards(): lax.psum_scatter(v, 'dp', scatter_dimension=v.ndim - 2, tiled=True)]
    reduce_sum x27 -> x3, other arithmetic: 46.3 us -> 5.6 us  [the longest x1 2.86 us: shards(): tv = jnp.sum(jnp.where(tflag, dx, 0.0), 0)]
    psum x2 -> x1, blocking collectives: 103 us -> 63.9 us  [shards(): lax.psum((qgl, goutl[:, :96].T, gupl, gdnl.T, cs[0::2], csl[0::2], bst[0]...]
    dynamic_slice x36 -> x0, local copies, waits for them, and re-layouts: 27.5 us -> none  [shards(): text_att, layout_att, log_total = lax.map(page_forward, page_inputs)]
  transfers between devices with their start and end apart: 8 -> 20, of which waited for: 8 -> 9; matrix products, arithmetic and copies ran while one was open for 5% -> 5% of each run, Pallas kernels for 0% -> 12%
where the time goes in v1:
time: 703 us; the launch traced here: 700 us
  waiting for transfers between devices  349 us (50%)
  Pallas kernels  199 us (28%)
  blocking collectives  63.9 us (9%)
  local copies, waits for them, and re-layouts  33.4 us (5%)
  matrix products  16.7 us (2%)
  between operations  15.2 us (2%)
  other arithmetic  11.6 us (2%)
  starting transfers between devices  10.6 us (2%)
    reduce_scatter x3, waiting for transfers between devices, shards(): lax.psum_scatter(v, 'dp', scatter_dimension=v.ndim - 2, tiled=True)  217 us
    pallas_call x1, Pallas kernels, ffn(): pl.pallas_call(ffn_kernel, grid_spec=pltpu.PrefetchScalarGridSpec(num_sca...  83.7 us
    ppermute x4, waiting for transfers between devices, gather_pieces(): a = lax.ppermute(piece, 'mp', [(0, 1), (1, 0)])  72.8 us
    psum x1, blocking collectives, shards(): lax.psum((qgl, goutl[:, :96].T, gupl, gdnl.T, cs[0::2], csl[0::2], bst[0]...  63.9 us
    pallas_call x2, Pallas kernels, attn_bwd(): pl.pallas_call(functools.partial(attn_bwd_kernel, mode), grid_spec=pltpu....  48.8 us
    pallas_call x2, Pallas kernels, attn_fwd(): pl.pallas_call(attn_fwd_kernel, grid_spec=pltpu.PrefetchScalarGridSpec(nu...  37.3 us
    ppermute x4, waiting for transfers between devices, gather_pieces(): b = lax.ppermute(a, 'dp', cross(n))  37.1 us
    unnamed x5, waiting for transfers between devices  21.9 us
  transfers between devices with their start and end apart: 20, of which 9 were waited for; matrix products, arithmetic and copies ran while one was open for 5% of the time, Pallas kernels for 12%

profile of v1, /device:TPU:0, one launch (start us, length us, event | category | flops | bytes accessed | tf_op | source)
XLA Modules:
  0.0 699.7 jit_solution(2504426413003227497)
XLA Ops:
  7.2 2.2 pack.6
  9.4 3.0 collective-permute-start.8
  12.4 2.2 pack.7
  16.6 2.2 pack.4
  18.8 2.0 collective-permute-start
  22.5 72.8 %collective-permute-done.4.refs_0_ = f32[576,128]{1,0:T(8,128)} collective-permute-done((f32[576,128]{1,0:T(8,128)}, f32[576,128]{1,0:T(8,128)}, u32[]{:S(2)}, u32[]{:S(2)}) %collective-permute-start.4) | collective-permute-done | bytes 294944 | tf_op jit(solution)/shard_map/ppermute | solution.py:392
  99.8 2.5 collective-permute-done.5.refs_1_
  104.8 10.0 %collective-permute-done.1.pb = f32[2280,128]{1,0:T(8,128)} collective-permute-done((f32[2280,128]{1,0:T(8,128)}, f32[2280,128]{1,0:T(8,128)}, u32[]{:S(2)}, u32[]{:S(2)}) %collective-permute-start.1) | collective-permute-done | bytes 1167392 | tf_op jit(solution)/shard_map/ppermute | solution.py:393
  115.5 11.9 %collective-permute-done.9.refs_1_ = f32[2304,128]{1,0:T(8,128)} collective-permute-done((f32[2304,128]{1,0:T(8,128)}, f32[2304,128]{1,0:T(8,128)}, u32[]{:S(2)}, u32[]{:S(2)}) %collective-permute-start.9) | collective-permute-done | bytes 1179680 | tf_op jit(solution)/shard_map/ppermute | solution.py:393
  127.5 12.6 %collective-permute-done.13.refs_1_ = f32[2304,128]{1,0:T(8,128)} collective-permute-done((f32[2304,128]{1,0:T(8,128)}, f32[2304,128]{1,0:T(8,128)}, u32[]{:S(2)}, u32[]{:S(2)}) %collective-permute-start.13) | collective-permute-done | bytes 1179680 | tf_op jit(solution)/shard_map/ppermute | solution.py:393
  141.5 2.2 copy.61.cl
  148.4 18.7 %attn_fwd.2 = (bf16[1536,384]{1,0:T(8,128)(2,1)}, bf16[1536,384]{1,0:T(8,128)(2,1)}, bf16[1536,384]{1,0:T(8,128)(2,1)}, bf16[1536,128]{1,0:T(8,128)(2,1)}, bf16[...) custom-call(s32[3]{0:T(128)} %len_ref.7, ...), custom_call_target="tpu_custom_call" | custom-call | tf_op jit(solution)/shard_map/attn_fwd/pallas_call | solution.py:60
  167.1 3.3 unpack.3.outw
  170.3 4.8 unpack_first.1
  175.1 18.6 %attn_fwd.3 = (bf16[1536,384]{1,0:T(8,128)(2,1)}, bf16[1536,384]{1,0:T(8,128)(2,1)}, bf16[1536,384]{1,0:T(8,128)(2,1)}, bf16[1536,128]{1,0:T(8,128)(2,1)}, bf16[...) custom-call(s32[3]{0:T(128)} %len_ref.7, ...), custom_call_target="tpu_custom_call" | custom-call | tf_op jit(solution)/shard_map/attn_fwd/pallas_call | solution.py:60
  193.9 6.7 unpack.4.up
  200.6 6.4 unpack.5.down
  206.9 83.7 %middle.1 = (f32[1536,768]{1,0:T(8,128)}, f32[1536,192]{1,0:T(8,128)}, f32[1536,768]{1,0:T(8,128)}, f32[1536,192]{1,0:T(8,128)}, bf16[2,1536,384]{2,1,0:T(8,128)...) custom-call(s32[1]{0:T(128)} %bitcast.mp_ref, ...), custom_call_target="tpu_custom_call" | custom-call | tf_op jit(solution)/shard_map/middle/pallas_call | solution.py:248
  290.7 3.4 dynamic-slice_bitcast_fusion.1
  295.0 24.2 %attn_bwd2.2 = (bf16[3,1536,384]{2,1,0:T(8,128)(2,1)}, bf16[3,1536,128]{2,1,0:T(8,128)(2,1)}) custom-call(s32[3]{0:T(128)} %len_ref.7, bf16[1536,384]{1,0:T(8,128)(2,1)} %get-tuple-element.84.qt_ref, bf16[1536,384]{1,0:T(8,128)(2,1)} %get-tuple-element.85.kt_ref, bf16[1536,384]{1,0:T(8,128)(2,1)} %get-tuple-element.86.vt_ref, ...), custom_call_target="tpu_custom_call" | custom-call | tf_op jit(solution)/shard_map/attn_bwd2/pallas_call | solution.py:156
  319.3 6.8 fusion.5
  326.0 6.4 copy.65
  337.8 2.5 convert_reduce_fusion
  340.6 24.6 %attn_bwd2.3 = (bf16[3,1536,384]{2,1,0:T(8,128)(2,1)}, bf16[3,1536,128]{2,1,0:T(8,128)(2,1)}) custom-call(s32[3]{0:T(128)} %len_ref.7, bf16[1536,384]{1,0:T(8,128)(2,1)} %get-tuple-element.94.qt_ref, bf16[1536,384]{1,0:T(8,128)(2,1)} %get-tuple-element.95.kt_ref, bf16[1536,384]{1,0:T(8,128)(2,1)} %get-tuple-element.96.vt_ref, ...), custom_call_target="tpu_custom_call" | custom-call | tf_op jit(solution)/shard_map/attn_bwd2/pallas_call | solution.py:156
  370.1 3.3 fusion.13
  373.5 3.3 fusion.14
  376.8 2.9 select_reduce_fusion
  379.7 63.9 %all-reduce.3 = (f32[768]{0:T(1024)}, f32[192]{0:T(256)}, f32[2,384]{1,0:T(2,128)}, f32[6,768]{1,0:T(8,128)S(1)}, f32[1536]{0:T(1024)}, /*index=5*/f32[2,96]{1,0:T(2,128)}, f32[6,192]{1,0:T(8,128)S(1)}, f32[384]{0:T(512)}) all-reduce(f32[768]{0:T(1024)S(1)} %get-tuple-element.173, ...), channel_id=1, replica_groups=mesh['dp'=16,'mp'=2] {'dp'}, use_global_device_ids=true, to_apply=%region_1.2 | all-reduce | flops 9600 | bytes 76800 | tf_op jit(solution)/shard_map/psum | solution.py:449
  448.9 20.0 %all-reduce.7.cloned.1.call-done = (f32[3,768,384]{2,0,1:T(4,128)}, f32[3,192,96]{2,1,0:T(8,128)}, f32[96,192]{0,1:T(8,128)}, f32[192,384]{1,0:T(8,128)}, f32[384,192]{0,1:T(8,128)}) async-done(((f32[3,768,384]{2,0,1:T(4,128)}, f32[3,192,96]{2,1,0:T(8,128)}, f32[96,192]{0,1:T(8,128)}, f32[192,384]{1,0:T(8,128)}, f32[384,192]{0,1:T(8,128)}), (f32[3,768,384]{2,0,1:T(4,128)}, f32[3,192,96]{2,1,0:T(8,128)}, ...) | async-done | bytes 4423696
  472.3 59.1 %reduce-scatter.4.cloned.1.call-done = f32[48,384]{1,0:T(8,128)} async-done(((f32[768,384]{1,0:T(8,128)}), f32[48,384]{1,0:T(8,128)}) %reduce-scatter.4.cloned.1.call-update) | async-done | bytes 73744 | tf_op jit(solution)/shard_map/reduce_scatter | solution.py:434
  531.4 79.0 %reduce-scatter.8.cloned.1.call-done = f32[48,1536]{1,0:T(8,128)} async-done(((f32[768,1536]{1,0:T(8,128)}), f32[48,1536]{1,0:T(8,128)}) %reduce-scatter.8.cloned.1.call-update) | async-done | bytes 294928 | tf_op jit(solution)/shard_map/reduce_scatter | solution.py:434
  610.4 79.4 %reduce-scatter.6.cloned.1.call-done = f32[48,1536]{1,0:T(8,128)} async-done(((f32[768,1536]{1,0:T(8,128)}), f32[48,1536]{1,0:T(8,128)}) %reduce-scatter.6.cloned.1.call-update) | async-done | bytes 294928 | tf_op jit(solution)/shard_map/reduce_scatter | solution.py:434
  (162 shorter events, 40.1 us)
Async XLA Ops:
  7.2 461.7 %all-reduce.7.cloned.1.call-start = ((), (), s32[]{:S(2)}) async-start(), calls=%async_computation.6 | async-start | bytes 11403264
  9.4 87.9 %collective-permute-start.8 = (f32[2304,128]{1,0:T(8,128)}, f32[2304,128]{1,0:T(8,128)}, u32[]{:S(2)}, u32[]{:S(2)}) collective-permute-start(f32[2304,128]{1,0:T(8,128)} %pack.6), channel_id=1, source_target_pairs={{0,1},{1,0},{2,3},{3,2},{4,5},{5,4},{6,7},{7,6},{8,9},{9,8},{10,11... | collective-permute-start | bytes 3538952 | tf_op jit(solution)/shard_map/ppermute | solution.py:392
  14.5 84.5 %collective-permute-start.12 = (f32[2304,128]{1,0:T(8,128)}, f32[2304,128]{1,0:T(8,128)}, u32[]{:S(2)}, u32[]{:S(2)}) collective-permute-start(f32[2304,128]{1,0:T(8,128)} %pack.7), channel_id=1, source_target_pairs={{0,1},{1,0},{2,3},{3,2},{4,5},{5,4},{6,7},{7,6},{8,9},{9,8},{10,11... | collective-permute-start | bytes 3538952 | tf_op jit(solution)/shard_map/ppermute | solution.py:392
  16.6 82.8 %copy-start.25 = (s32[1536]{0:T(1024)S(1)}, s32[1536]{0:T(1024)}, u32[]{:S(2)}) copy-start(s32[1536]{0:T(1024)} %param.28) | copy-start | bytes 18436
  16.6 82.8 %copy-start.12 = (bf16[1536,192]{0,1:T(8,128)(2,1)S(1)}, bf16[1536,192]{0,1:T(8,128)(2,1)}, u32[]{:S(2)}) copy-start(bf16[1536,192]{0,1:T(8,128)(2,1)} %param.26) | copy-start | bytes 1769476
  18.8 83.6 %copy-start.36 = (bf16[192]{0:T(256)(128)(2,1)S(1)}, bf16[192]{0:T(256)(128)(2,1)}, u32[]{:S(2)}) copy-start(bf16[192]{0:T(256)(128)(2,1)} %param.31) | copy-start | bytes 1156
  18.8 84.8 %copy-start.21 = (bf16[2,384]{1,0:T(2,128)(2,1)S(1)}, bf16[2,384]{1,0:T(2,128)(2,1)}, u32[]{:S(2)}) copy-start(bf16[2,384]{1,0:T(2,128)(2,1)} %refs_5_.1) | copy-start | bytes 4612
  18.8 96.1 %copy-start.28 = (bf16[2,96]{1,0:T(2,128)(2,1)S(1)}, bf16[2,96]{1,0:T(2,128)(2,1)}, u32[]{:S(2)}) copy-start(bf16[2,96]{1,0:T(2,128)(2,1)} %refs_6_.1) | copy-start | bytes 1156
  18.8 122.0 %copy-start.9 = (bf16[3,192,96]{2,1,0:T(8,128)(2,1)S(1)}, bf16[3,192,96]{2,1,0:T(8,128)(2,1)}, u32[]{:S(2)}) copy-start(bf16[3,192,96]{2,1,0:T(8,128)(2,1)} %refs_1_.1) | copy-start | bytes 331780
  18.8 78.2 %collective-permute-start = (f32[2280,128]{1,0:T(8,128)}, f32[2280,128]{1,0:T(8,128)}, u32[]{:S(2)}, u32[]{:S(2)}) collective-permute-start(f32[2280,128]{1,0:T(8,128)} %pack.4), channel_id=1, source_target_pairs={{0,1},{1,0},{2,3},{3,2},{4,5},{5,4},{6,7},{7,6},{8,9},{9,8},{10,11... | collective-permute-start | bytes 3502088 | tf_op jit(solution)/shard_map/ppermute | solution.py:392
  22.5 72.8 %collective-permute-start.4 = (f32[576,128]{1,0:T(8,128)}, f32[576,128]{1,0:T(8,128)}, u32[]{:S(2)}, u32[]{:S(2)}) collective-permute-start(f32[576,128]{1,0:T(8,128)} %pack.5), channel_id=1, source_target_pairs={{0,1},{1,0},{2,3},{3,2},{4,5},{5,4},{6,7},{7,6},{8,9},{9,8},{10,11... | collective-permute-start | bytes 884744 | tf_op jit(solution)/shard_map/ppermute | solution.py:392
  95.3 7.0 %collective-permute-start.5 = (f32[576,128]{1,0:T(8,128)}, f32[576,128]{1,0:T(8,128)}, u32[]{:S(2)}, u32[]{:S(2)}) collective-permute-start(f32[576,128]{1,0:T(8,128)} %collective-permute-done.4.refs_0_), channel_id=1, source_target_pairs={{0,4},{2,10},{4,0},{6,14},{8,12},{10,2},{12,8},{14,6},{16,20},{18,... | collective-permute-start | bytes 884744 | tf_op jit(solution)/shard_map/ppermute | solution.py:393
  97.0 17.8 %collective-permute-start.1 = (f32[2280,128]{1,0:T(8,128)}, f32[2280,128]{1,0:T(8,128)}, u32[]{:S(2)}, u32[]{:S(2)}) collective-permute-start(f32[2280,128]{1,0:T(8,128)} %collective-permute-done.pa), channel_id=1, source_target_pairs={{0,4},{2,10},{4,0},{6,14},{8,12},{10,2},{12,8},{14,6},{16,20},{18,... | collective-permute-start | bytes 3502088 | tf_op jit(solution)/shard_map/ppermute | solution.py:393
  97.3 30.2 %collective-permute-start.9 = (f32[2304,128]{1,0:T(8,128)}, f32[2304,128]{1,0:T(8,128)}, u32[]{:S(2)}, u32[]{:S(2)}) collective-permute-start(f32[2304,128]{1,0:T(8,128)} %collective-permute-done.8.refs_0_), channel_id=1, source_target_pairs={{0,4},{2,10},{4,0},{6,14},{8,12},{10,2},{12,8},{14,6},{16,20},{18,... | collective-permute-start | bytes 3538952 | tf_op jit(solution)/shard_map/ppermute | solution.py:393
  99.0 41.1 %collective-permute-start.13 = (f32[2304,128]{1,0:T(8,128)}, f32[2304,128]{1,0:T(8,128)}, u32[]{:S(2)}, u32[]{:S(2)}) collective-permute-start(f32[2304,128]{1,0:T(8,128)} %collective-permute-done.12.refs_0_), channel_id=1, source_target_pairs={{0,4},{2,10},{4,0},{6,14},{8,12},{10,2},{12,8},{14,6},{16,20},{18,... | collective-permute-start | bytes 3538952 | tf_op jit(solution)/shard_map/ppermute | solution.py:393
  99.7 47.0 %copy-start.26 = (s32[1536]{0:T(1024)S(1)}, s32[1536]{0:T(1024)}, u32[]{:S(2)}) copy-start(s32[1536]{0:T(1024)} %param.27) | copy-start | bytes 18436
  99.7 47.0 %copy-start.5 = (bf16[1536,768]{1,0:T(8,128)(2,1)S(1)}, bf16[1536,768]{1,0:T(8,128)(2,1)}, u32[]{:S(2)}) copy-start(bf16[1536,768]{1,0:T(8,128)(2,1)} %param.25) | copy-start | bytes 7077892
  99.7 47.0 %copy-start.33 = (bf16[768]{0:T(1024)(128)(2,1)S(1)}, bf16[768]{0:T(1024)(128)(2,1)}, u32[]{:S(2)}) copy-start(bf16[768]{0:T(1024)(128)(2,1)} %param.30) | copy-start | bytes 4612
  99.7 3.8 collective-permute-start.6
  102.3 13.1 %collective-permute-start.2 = (f32[2280,128]{1,0:T(8,128)}, f32[2280,128]{1,0:T(8,128)}, u32[]{:S(2)}, u32[]{:S(2)}) collective-permute-start(f32[2280,128]{1,0:T(8,128)} %collective-permute-done.pa), channel_id=1, source_target_pairs={{0,2},{2,0},{4,6},{6,4},{8,10},{10,8},{12,14},{14,12},{16,18},{18,... | collective-permute-start | bytes 3502088 | tf_op jit(solution)/shard_map/ppermute | solution.py:394
  103.6 11.3 %collective-permute-start.7 = (f32[576,128]{1,0:T(8,128)}, f32[576,128]{1,0:T(8,128)S(1)}, u32[]{:S(2)}, u32[]{:S(2)}) collective-permute-start(f32[576,128]{1,0:T(8,128)} %collective-permute-done.5.refs_1_), channel_id=1, source_target_pairs={{0,2},{2,0},{4,6},{6,4},{8,10},{10,8},{12,14},{14,12},{16,18},{18,... | collective-permute-start | bytes 884744 | tf_op jit(solution)/shard_map/ppermute | solution.py:395
  114.8 55.5 %collective-permute-start.3 = (f32[2280,128]{1,0:T(8,128)}, f32[2280,128]{1,0:T(8,128)}, u32[]{:S(2)}, u32[]{:S(2)}) collective-permute-start(f32[2280,128]{1,0:T(8,128)} %collective-permute-done.1.pb), channel_id=1, source_target_pairs={{0,2},{2,0},{4,6},{6,4},{8,10},{10,8},{12,14},{14,12},{16,18},{18,... | collective-permute-start | bytes 3502088 | tf_op jit(solution)/shard_map/ppermute | solution.py:395
  114.9 79.0 %collective-permute-start.10 = (f32[2304,128]{1,0:T(8,128)}, f32[2304,128]{1,0:T(8,128)}, u32[]{:S(2)}, u32[]{:S(2)}) collective-permute-start(f32[2304,128]{1,0:T(8,128)} %collective-permute-done.8.refs_0_), channel_id=1, source_target_pairs={{0,2},{2,0},{4,6},{6,4},{8,10},{10,8},{12,14},{14,12},{16,18},{18,... | collective-permute-start | bytes 3538952 | tf_op jit(solution)/shard_map/ppermute | solution.py:394
  115.4 85.1 %collective-permute-start.14 = (f32[2304,128]{1,0:T(8,128)}, f32[2304,128]{1,0:T(8,128)}, u32[]{:S(2)}, u32[]{:S(2)}) collective-permute-start(f32[2304,128]{1,0:T(8,128)} %collective-permute-done.12.refs_0_), channel_id=1, source_target_pairs={{0,2},{2,0},{4,6},{6,4},{8,10},{10,8},{12,14},{14,12},{16,18},{18,... | collective-permute-start | bytes 3538952 | tf_op jit(solution)/shard_map/ppermute | solution.py:394
  127.5 66.4 %collective-permute-start.11 = (f32[2304,128]{1,0:T(8,128)}, f32[2304,128]{1,0:T(8,128)}, u32[]{:S(2)}, u32[]{:S(2)}) collective-permute-start(f32[2304,128]{1,0:T(8,128)} %collective-permute-done.9.refs_1_), channel_id=1, source_target_pairs={{0,2},{2,0},{4,6},{6,4},{8,10},{10,8},{12,14},{14,12},{16,18},{18,... | collective-permute-start | bytes 3538952 | tf_op jit(solution)/shard_map/ppermute | solution.py:395
  140.1 60.5 %collective-permute-start.15 = (f32[2304,128]{1,0:T(8,128)}, f32[2304,128]{1,0:T(8,128)}, u32[]{:S(2)}, u32[]{:S(2)}) collective-permute-start(f32[2304,128]{1,0:T(8,128)} %collective-permute-done.13.refs_1_), channel_id=1, source_target_pairs={{0,2},{2,0},{4,6},{6,4},{8,10},{10,8},{12,14},{14,12},{16,18},{18,... | collective-permute-start | bytes 3538952 | tf_op jit(solution)/shard_map/ppermute | solution.py:395
  334.4 197.0 %reduce-scatter.4.cloned.1.call-start = ((), (), s32[]{:S(2)}) async-start(), calls=%async_computation.3 | async-start | bytes 1253376 | tf_op jit(solution)/shard_map/reduce_scatter | solution.py:434
  335.1 275.2 %reduce-scatter.8.cloned.1.call-start = ((), (), s32[]{:S(2)}) async-start(), calls=%async_computation.5 | async-start | bytes 5013504 | tf_op jit(solution)/shard_map/reduce_scatter | solution.py:434
  335.9 353.9 %reduce-scatter.6.cloned.1.call-start = ((), (), s32[]{:S(2)}) async-start(), calls=%async_computation.4 | async-start | bytes 5013504 | tf_op jit(solution)/shard_map/reduce_scatter | solution.py:434
  379.7 67.7 %copy-start.7 = (f32[1536,192]{1,0:T(8,128)S(1)}, f32[1536,192]{1,0:T(8,128)}, u32[]{:S(2)}) copy-start(f32[1536,192]{1,0:T(8,128)} %get-tuple-element.139) | copy-start | bytes 3538948
  468.9 222.6 %copy-start.16 = (f32[192,384]{1,0:T(8,128)S(1)}, f32[192,384]{1,0:T(8,128)}, u32[]{:S(2)}) copy-start(f32[192,384]{1,0:T(8,128)} %get-tuple-element.204) | copy-start | bytes 884740
  468.9 223.3 %copy-start.15 = (f32[384,192]{0,1:T(8,128)S(1)}, f32[384,192]{0,1:T(8,128)}, u32[]{:S(2)}) copy-start(f32[384,192]{0,1:T(8,128)} %get-tuple-element.206) | copy-start | bytes 884740
  (29 other events, 357.9 us)
Sparse Core Ops, SparseCore 0:
  334.5 134.3 all-reduce.6
  473.1 58.2 reduce-scatter.3
  535.8 74.5 reduce-scatter.7
  615.1 74.5 reduce-scatter.5

commit v2 on v1

v2 whole, which is shorter than its diff:
```python
import functools
import jax, jax.numpy as jnp
from jax import lax
from jax.experimental import pallas as pl
from jax.experimental.pallas import tpu as pltpu
F32=jnp.float32; BF=jnp.bfloat16
NT=(((1,),(1,)),((),()))
TN=(((0,),(0,)),((),()))
def dot(a,b): return jnp.dot(a,b,preferred_element_type=F32)
def dotg(a,b,dn): return lax.dot_general(a,b,dn,preferred_element_type=F32)
VLIM=60*1024*1024

def cost(us): return pl.CostEstimate(flops=int(us*1e7),bytes_accessed=1024,transcendentals=0)

def lane_iota(shape): return lax.broadcasted_iota(jnp.int32,shape,len(shape)-1)

def attn_fwd_kernel(first, len_ref, half_ref, xt_ref, xl_ref, wt_ref, wl_ref, bt_ref, bl_ref, *rest):
    qt_ref, kt_ref, vt_ref, ql_ref, kl_ref, vl_ref, ot_ref, ol_ref, lse_ref, olT, lseT=rest[-11:]
    page=first+pl.program_id(0)
    seq=xt_ref.shape[0]
    xt=xt_ref[...]; xl=xl_ref[...]
    for c,(t,l) in enumerate(((qt_ref,ql_ref),(kt_ref,kl_ref),(vt_ref,vl_ref))):
        t[...]=(dot(xt,wt_ref[c])+bt_ref[c:c+1,:]).astype(BF)
        l[...]=(dot(xl,wl_ref[c])+bl_ref[c:c+1,:]).astype(BF)
    lane=lane_iota((seq,128))
    row=lax.broadcasted_iota(jnp.int32,(seq,128),0)
    length=len_ref[page]
    bias=jnp.where(row<length,0.0,-1e9).astype(BF)
    one=jnp.ones((seq,128),BF)
    ql=jnp.where(lane==96,one,ql_ref[...]*BF(0.25))
    kl=jnp.where(lane==96,bias,kl_ref[...])
    vlT=vl_ref[...].T
    zero=jnp.zeros((seq,128),BF)
    olT[...]=jnp.zeros_like(olT); lseT[...]=jnp.zeros_like(lseT)
    for j in range(3):
        cols=slice(128*j,128*j+128)
        qbig=jnp.concatenate([qt_ref[:,cols]*BF(0.125),ql],1)
        vT=vt_ref[:,cols].T
        halves=[]
        for s in range(2):
            h=2*j+s
            kbig=jnp.concatenate([jnp.where(lane//64==s,kt_ref[:,cols],zero),
                                  jnp.where((lane//16==h)|(lane==96),kl,zero)],1)
            S=dotg(kbig,qbig,NT)
            m=jnp.max(S,0,keepdims=True)
            e=jnp.exp(S-m)
            ssum=jnp.sum(e,0,keepdims=True)
            v80=jnp.concatenate([vT[64*s:64*s+64],vlT[16*h:16*h+16]],0)
            o=dot(v80,e.astype(BF))*(1.0/ssum)
            halves.append(o[:64])
            olT[16*h:16*h+16,:]=o[64:]
            lseT[h:h+1,:]=m+jnp.log(ssum)
        ot_ref[:,cols]=jnp.concatenate(halves,0).T.astype(BF)
    ol_ref[...]=olT[...].T.astype(BF)
    lse_ref[...]=pltpu.roll(lseT[...].T,97,1)

def attn_fwd(first, count, lengths, half, xt, xl, wt, wl, bt, bl, prev):
    rows=xt.shape[0]; pages=lengths.shape[0]; seq=rows//pages
    rb=lambda n: pl.BlockSpec((seq,n),lambda p,*_:(first+p,0))
    full=lambda a: pl.BlockSpec((None,)*(a.ndim-3)+a.shape[-3:],lambda p,l,h:(h[0],0,0,0)[4-a.ndim:]) if a.ndim>2 else pl.BlockSpec(a.shape,lambda p,*_:(0,0))
    whole=pl.BlockSpec(memory_space=pl.ANY)
    o=lambda n,d=BF: jax.ShapeDtypeStruct((rows,n),d)
    return pl.pallas_call(functools.partial(attn_fwd_kernel,first),
        grid_spec=pltpu.PrefetchScalarGridSpec(num_scalar_prefetch=2,grid=(count,),
            in_specs=[rb(768),rb(192),full(wt),full(wl),full(bt),full(bl)]+[whole]*len(prev),
            out_specs=[rb(384)]*3+[rb(128)]*3+[rb(384),rb(128),rb(128)],
            scratch_shapes=[pltpu.VMEM((128,seq),F32),pltpu.VMEM((128,seq),F32)]),
        out_shape=[o(384)]*3+[o(128)]*3+[o(384),o(128),o(128,F32)],
        input_output_aliases={8+i:i for i in range(len(prev))},
        compiler_params=pltpu.CompilerParams(vmem_limit_bytes=VLIM),cost_estimate=cost(6.2*count),name="attn_fwd")(lengths,half,xt,xl,wt,wl,bt,bl,*prev)

def ind_matrix(j):
    r=lax.broadcasted_iota(jnp.int32,(256,128),0)%128
    l=lax.broadcasted_iota(jnp.int32,(256,128),1)
    h=(r//64+2*j) if j is not None else r//16
    return jnp.where((l==97+h)&(h<6),1.0,0.0).astype(BF)

def split2(v):
    hi=v.astype(BF)
    return hi,(v-hi.astype(F32)).astype(BF)

def bwd_page(length, qt_ref, kt_ref, vt_ref, ql_ref, kl_ref, vl_ref, ot_ref, ol_ref, lse_ref, dot_ref, dol_ref,
                    dpt_ref, dpl_ref, dqlT):
    seq=qt_ref.shape[0]
    lane=lane_iota((seq,128))
    row=lax.broadcasted_iota(jnp.int32,(seq,128),0)
    bias=jnp.where(row<length,0.0,-1e9).astype(BF)
    zero=jnp.zeros((seq,128),BF); one=jnp.ones((seq,128),BF)
    nl=-lse_ref[...]
    hi=nl.astype(BF); r1=nl-hi.astype(F32); mid=r1.astype(BF); lo=r1-mid.astype(F32)
    ext=hi+pltpu.roll(mid.astype(F32),7,1).astype(BF)+pltpu.roll(lo,14,1).astype(BF)
    qle=jnp.where(lane<96,ql_ref[...]*BF(0.25),jnp.where(lane==96,one,ext))
    kl=kl_ref[...]; vl=vl_ref[...]; ql=ql_ref[...]
    klT=kl.T
    dqlT[...]=jnp.zeros_like(dqlT)
    def sums(a,b,m):
        p=a.astype(F32)*b.astype(F32)
        h_,l_=split2(p)
        return dot(jnp.concatenate([h_,l_],1),m)
    dol=dol_ref[...]
    d_l=sums(dol,ol_ref[...],ind_matrix(None))
    d_t=d_l
    for j in range(3):
        cols=slice(128*j,128*j+128)
        d_t=d_t+sums(dot_ref[:,cols],ot_ref[:,cols],ind_matrix(j))
    def ext_delta(d):
        h_=d.astype(BF); l_=d-h_.astype(F32)
        return h_+pltpu.roll(l_,7,1).astype(BF)
    dol1=jnp.where(lane<96,dol*BF(0.125),ext_delta(d_t*-0.125))
    dol2=jnp.where(lane<96,dol*BF(0.25),ext_delta(d_l*-0.25))
    for j in range(3):
        cols=slice(128*j,128*j+128)
        qt=qt_ref[:,cols]; kt=kt_ref[:,cols]; vt=vt_ref[:,cols]; dO=dot_ref[:,cols]
        qbig=jnp.concatenate([qt*BF(0.125),qle],1)
        dbig=jnp.concatenate([dO*BF(0.125),dol1],1)
        dObig=jnp.concatenate([dO,dol],1)
        prev=None
        ktT=kt.T
        for s in range(2):
            h=2*j+s
            tm=lane//64==s; lm=lane//16==h
            kbig=jnp.concatenate([jnp.where(tm,kt,zero),jnp.where(lm,kl,jnp.where(lane==96,bias,
                 jnp.where((lane==97+h)|(lane==104+h)|(lane==111+h),one,zero)))],1)
            vle=jnp.where(lm,vl,jnp.where((lane==97+h)|(lane==104+h),one,zero))
            vbig=jnp.concatenate([jnp.where(tm,vt,zero),vle],1)
            S=dotg(kbig,qbig,NT)
            M1=dotg(vbig,dbig,NT)
            M2=dotg(vle,dol2,NT)
            Pm=jnp.exp(S)
            Pb=Pm.astype(BF)
            R1=(Pm*M1).astype(BF)
            R2=(Pm*M2).astype(BF)
            dk_t=dot(R1,qt); dk_l=dot(R2,ql); dv=dot(Pb,dObig)
            dq_t=dot(ktT[64*s:64*s+64],R1)
            dq_l=dot(klT[16*h:16*h+16],R2)
            cur=(dq_t,dk_t,dv[:,:128])
            curl=(dq_l,dk_l,dv[:,128:])
            dqlT[16*h:16*h+16,:]=dq_l
            if s==1:
                dpt_ref[0,:,cols]=jnp.concatenate([prev[0],dq_t],0).T.astype(BF)
            for c in range(1,3):
                if s==1:
                    dpt_ref[c,:,cols]=jnp.where(lane<64,prev[c],cur[c]).astype(BF)
                pv=jnp.zeros((seq,128),BF) if h==0 else dpl_ref[c]
                dpl_ref[c]=jnp.where(lm,curl[c].astype(BF),pv)
            prev=cur
    dpl_ref[0]=dqlT[...].T.astype(BF)

def bwd_kernel(first, len_ref, half_ref, qt, kt, vt, ql, kl, vl, ot, ol, lse, dO, dOl, *rest):
    dpt,dpl,dqlT=rest[-3:]
    bwd_page(len_ref[first+pl.program_id(0)],qt,kt,vt,ql,kl,vl,ot,ol,lse,dO.at[0],dOl.at[0],dpt,dpl,dqlT)


def attn_bwd(first,count,lengths,half,saved,dO,dOl,prev):
    rows=saved[0].shape[0]; seq=rows//lengths.shape[0]
    rb=lambda n: pl.BlockSpec((seq,n),lambda i,*_:(first+i,0))
    hb=lambda n: pl.BlockSpec((1,seq,n),lambda i,l,h:(h[0],first+i,0))
    pb=lambda n: pl.BlockSpec((3,seq,n),lambda i,l,h:(h[0],first+i,0))
    whole=pl.BlockSpec(memory_space=pl.ANY)
    return pl.pallas_call(functools.partial(bwd_kernel,first),
        grid_spec=pltpu.PrefetchScalarGridSpec(num_scalar_prefetch=2,grid=(count,),
            in_specs=[rb(384)]*3+[rb(128)]*3+[rb(384),rb(128),rb(128),hb(384),hb(128)]+[whole]*len(prev),
            out_specs=[pb(384),pb(128)],scratch_shapes=[pltpu.VMEM((128,seq),F32)]),
        out_shape=[jax.ShapeDtypeStruct((6,rows,384),BF),jax.ShapeDtypeStruct((6,rows,128),BF)],
        input_output_aliases={13+i:i for i in range(len(prev))},
        compiler_params=pltpu.CompilerParams(vmem_limit_bytes=VLIM),cost_estimate=cost(9*count),name="attn_bwd")(lengths,half,*saved,dO,dOl,*prev)


def dx_kernel(dpt, dpl, wt, wl, dr1, dr1l, tm, lm, dx, dxl, wts, wls):
    @pl.when(pl.program_id(0)==0)
    def _():
        for h in range(2):
            for c in range(3):
                i=3*h+c
                wts[:,384*i:384*i+384]=wt[h,c]
                wls[:,128*i:128*i+128]=wl[h,c]
    def back(d,w,base,flag):
        v=dotg(jnp.concatenate([d[i] for i in range(6)],1),w[...],NT)+base[...]
        return jnp.where(flag[...]==1,0.0,v)
    dx[...]=back(dpt,wts,dr1,tm)
    dxl[...]=back(dpl,wls,dr1l,lm).T


def input_grad(tile,dp,wts,dr1,dr1l,tm,lm):
    rows=dr1.shape[0]
    rb=lambda n: pl.BlockSpec((tile,n),lambda i:(i,0))
    pb=lambda n: pl.BlockSpec((6,tile,n),lambda i:(0,i,0))
    full=lambda a: pl.BlockSpec(a.shape,lambda i:(0,0,0,0))
    return pl.pallas_call(dx_kernel,grid=(rows//tile,),
        in_specs=[pb(384),pb(128)]+[full(w) for w in wts]+[rb(768),rb(192),rb(1),rb(1)],
        out_specs=[rb(768),pl.BlockSpec((192,tile),lambda i:(0,i))],
        scratch_shapes=[pltpu.VMEM((768,2304),BF),pltpu.VMEM((192,768),BF)],
        out_shape=[jax.ShapeDtypeStruct((rows,768),F32),jax.ShapeDtypeStruct((192,rows),F32)],
        compiler_params=pltpu.CompilerParams(vmem_limit_bytes=VLIM),cost_estimate=cost(5),name="input_grad")(*dp,*wts,dr1,dr1l,tm,lm)


def place_blocks(acc, keep, send, sem, position, n):
    if n!=16:
        cp=pltpu.make_async_copy(acc,keep,sem); cp.start(); cp.wait()
        return
    c=position&1; x=(position>>1)&1; z0=(position>>2)&1; z1=(position>>3)&1
    rows=acc.shape[0]//16
    copies=[]
    for out,core in ((keep,c),(send,1-c)):
        for q in range(8):
            r2,r3,r4=q>>2,(q>>1)&1,q&1
            fx=jnp.where(core==0,r2,r3); fz=jnp.where(core==0,r3,r2)
            block=(z1^r4)*8+(z0^fz)*4+(x^fx)*2+core
            copies.append(pltpu.make_async_copy(acc.at[pl.ds(pl.multiple_of(block*rows,8),rows)],out.at[pl.ds(q*rows,rows)],sem))
    for cp in copies: cp.start()
    for cp in copies: cp.wait()


def block_shapes(rows,cols,n):
    S=jax.ShapeDtypeStruct
    if n!=16: return [S((rows,cols),F32),S((8,128),F32)]
    return [S((rows//2,cols),F32)]*2


def qkv_grad_kernel(n, pos_ref, xt, xl, dpt, dpl, sel, wt, wl, keep, send, acc, sums, suml, sem):
    x=xt[...]; s=sel[...]; xv=xl[...]
    def add(first):
        def put(ref,v):
            if first: ref[...]=v
            else: ref[...]+=v
        for c in range(3):
            put(acc.at[:,384*c:384*c+384],dotg(x,dpt[c],TN))
            put(acc.at[192*c:192*c+192,1152:],dotg(xv,dpl[c],TN))
            put(sums.at[c],dot(s,dpt[c])); put(suml.at[c],dot(s,dpl[c]))
    first=pl.program_id(0)==0
    pl.when(first)(lambda: add(True))
    pl.when(jnp.logical_not(first))(lambda: add(False))
    @pl.when(pl.program_id(0)==pl.num_programs(0)-1)
    def _():
        rest=[]
        t=jnp.zeros((8,768),F32); l=jnp.zeros((8,192),F32)
        for c in range(3):
            a=sums[c]; b=suml[c]
            rest.extend([a[:,128*j:128*j+128] for j in range(3)]+[b])
            for v,w,text in ((a,wt,True),(b,wl,False)):
                hi,lo=split2(v)
                lo2=(v-hi.astype(F32)-lo.astype(F32)).astype(BF)
                y=dotg(hi,w[0,c],NT)+dotg(lo,w[0,c],NT)+dotg(lo2,w[0,c],NT)
                if text: t=t+y
                else: l=l+y
        rest.extend([t[:,128*j:128*j+128] for j in range(6)]+[l[:,:128],jnp.concatenate([l[:,128:],jnp.zeros((8,64),F32)],1),jnp.zeros((32,128),F32)])
        acc[576:768,1152:]=jnp.concatenate(rest,0)
        place_blocks(acc,keep,send,sem,pos_ref[1],n)


def qkv_grad(n,pos,pages,xt,xl,dpt,dpl,sel,wt,wl):
    seq=xt.shape[0]//pages
    rb=lambda m: pl.BlockSpec((seq,m),lambda i,s:(i,0))
    pb=lambda m: pl.BlockSpec((3,seq,m),lambda i,s:(s[0],i,0))
    wb=lambda a: pl.BlockSpec((1,)+a.shape[1:],lambda i,s:(s[0],0,0,0))
    whole=pl.BlockSpec(memory_space=pl.ANY)
    return pl.pallas_call(functools.partial(qkv_grad_kernel,n),
        grid_spec=pltpu.PrefetchScalarGridSpec(num_scalar_prefetch=1,grid=(pages,),
            in_specs=[rb(768),rb(192),pb(384),pb(128),pl.BlockSpec((8,seq),lambda i,s:(0,i)),wb(wt),wb(wl)],
            out_specs=[whole,whole],
            scratch_shapes=[pltpu.VMEM((768,1280),F32),pltpu.VMEM((3,8,384),F32),pltpu.VMEM((3,8,128),F32),pltpu.SemaphoreType.DMA]),
        out_shape=block_shapes(768,1280,n),
        compiler_params=pltpu.CompilerParams(vmem_limit_bytes=VLIM),cost_estimate=cost(8),name="qkv_grad")(pos,xt,xl,dpt,dpl,sel,wt,wl)


EPS=1e-5
def gelu_parts(x):
    cdf=0.5+0.5*lax.erf(x*0.7071067811865476)
    phi=jnp.exp2(x*x*-0.7213475204444817-1.3257480647361593)
    return cdf, cdf+x*phi

def norm(v):
    mu=jnp.mean(v,-1,keepdims=True)
    c=v-mu
    inv=lax.rsqrt(jnp.mean(c*c,-1,keepdims=True)+EPS)
    return c*inv,inv

def norm_back(g,u,inv,gain):
    s=g*gain
    return inv*(s-jnp.mean(s,-1,keepdims=True)-u*jnp.mean(s*u,-1,keepdims=True))

def stream(own_col, own_off, x, o, o_own, cot, outw, up, down, shift, gain, upb, act, gp, out_ref, dr1_ref, dos, gup, gdn, gout, stat, bstat, first, chunk, flag, hook):
    d=x.shape[1]; F=up.shape[1]; half=F//2
    h1u,i1=norm(x.astype(F32)+dot(o,outw[...])+shift[2:3])
    h1=h1u*gain[0:1]+shift[0:1]
    h1b=h1.astype(BF)
    for f in range(0,F,chunk):
        cs=slice(f,f+chunk)
        pre=dot(h1b,up[:,cs])+upb[:,cs]
        cdf,der=gelu_parts(pre)
        act[:,cs]=(pre*cdf).astype(BF)
        gp[:,cs]=der.astype(BF)
    if hook is not None: hook()
    r2=h1+dot(act[...],down[...])+shift[3:4]
    u2,i2=norm(r2)
    y=u2*gain[1:2]+shift[1:2]
    out_ref[...]=y if out_ref.shape==y.shape else y.T
    g=cot.astype(F32)
    dr2=norm_back(g,u2,i2,gain[1:2])
    dr2b=dr2.astype(BF)
    for f in range(0,F,chunk):
        cs=slice(f,f+chunk)
        da=dotg(dr2b,down[cs,:],NT)
        gp[:,cs]=(da*gp[:,cs].astype(F32)).astype(BF)
    dh1=dotg(gp[...],up[...],NT)+dr2
    dr1=norm_back(dh1,h1u,i1,gain[0:1])
    dr1_ref[...]=dr1
    dr1b=dr1.astype(BF)
    dO=dotg(dr1b,outw[...],NT).astype(BF)
    w=dO.shape[1]//2
    dos[0]=dO[:,:w]; dos[1]=dO[:,w:]
    osl=pl.ds(pl.multiple_of(own_off,128),half)
    dpo=gp[:,osl]
    ones=jnp.ones((8,x.shape[0]),BF)
    rs=lambda v: jnp.sum(v,0,keepdims=True)
    st=jnp.concatenate([rs(dh1),rs(g),rs(dr1),rs(dr2),rs(dh1*h1u),rs(g*u2),rs(jnp.where(flag==1,dr1,0.0)),jnp.zeros((1,d),F32)],0)
    def put(first):
        for ref,a,b in ((gup,h1b,dpo),(gdn,dr2b,act[:,osl]),(gout,dr1b,o_own)):
            v=dotg(a,b,TN)
            if first: ref[...]=v
            else: ref[...]+=v
        b=dot(ones,dpo)
        if first:
            stat[...]=st; bstat[...]=b
        else:
            stat[...]+=st; bstat[...]+=b
    pl.when(first)(lambda: put(True))
    pl.when(jnp.logical_not(first))(lambda: put(False))

def ffn_kernel(n, s_ref, *refs):
    (xt, xl, oa, ob, ola, olb, ct, cl, tm, lm, sh, ga, shl, gal)=refs[:14]
    (up_own, outw_own, down_own, outl_own, upl_own, downl_own, upb_own, upbl_own)=refs[14:22]
    second=refs[22:30]; third=[refs[30+2*i:32+2*i] for i in range(4)]
    (to, lo, dr1, dr1l, dos, dosl, keep, send)=refs[38:46]
    (act, gp, actl, gpl, acc, up, outw, down, outwl, upl, downl, upb, upbl, st, bst, gupl, gdnl, goutl, stl, bstl, sem, sem_own, sem2, sem3)=refs[46:]
    mp=s_ref[0]; other=1-mp
    first=pl.program_id(0)==0
    half=lambda k,m: pl.ds(pl.multiple_of(k*m,m),m)
    column=lambda k: acc.at[:,128*k:128*k+128]
    own=[pltpu.make_async_copy(src,dst,sem_own.at[i]) for i,(src,dst) in enumerate((
        (outw_own,outw.at[half(mp,384),:]),(up_own,up.at[:,half(mp,1536)]),(down_own,down.at[half(mp,1536),:])))]
    two=[]; three=[]
    for i,src in enumerate(second):
        two.append([pltpu.make_async_copy(src.at[lo_:hi_],column(2*i+k).at[0:hi_-lo_],sem2.at[i,k]) for k,(lo_,hi_) in enumerate(((0,768),(768,1440)))])
    for i,src in enumerate(third):
        base=16+4*i if i<3 else 0
        three.append([pltpu.make_async_copy(src[s].at[r:r+m],column(base+k).at[d:d+m],sem3.at[i,q])
            for q,(s,r,k,d,m) in enumerate(((0,0,0,0,768),(0,768,1,0,384),(1,0,1,384,384),(1,384,2,0,768),(1,1152,3,0,400)))])
    @pl.when(first)
    def _():
        for cp in own: cp.start()
        for cps in two:
            for cp in cps: cp.start()
        for cps in three[:3]:
            for cp in cps: cp.start()
        for i,cps in enumerate(two):
            for cp in cps: cp.wait()
            p=s_ref[6+i]
            a,b=column(2*i),column(2*i+1)
            for j in range(12):
                src=a[96*j:96*j+96] if j<8 else b[96*(j-8):96*(j-8)+96]
                up[half(p,96),pl.ds(pl.multiple_of(other*1536+128*j,128),128)]=src.astype(BF)
            for j in range(6):
                outw[pl.ds(pl.multiple_of(other*384+p*48,16),48),128*j:128*j+128]=b[384+48*j:432+48*j].astype(BF)
        for cp in three[3]: cp.start()
        own[0].wait(); own[1].wait()
    def unpack_small():
        tail=[]
        for i in range(4):
            p=s_ref[2+i]
            v=column((16+4*i if i<3 else 0)+3)
            goutl[pl.ds(pl.multiple_of(p*24,8),24),:]=v[0:24]
            gdnl[pl.ds(pl.multiple_of(p*24,8),24),0:128]=v[24:48]
            for j in range(3):
                upl[pl.ds(pl.multiple_of(p*48,16),48),pl.ds(pl.multiple_of(other*384+128*j,128),128)]=v[48+48*j:96+48*j].astype(BF)
            rows=pl.ds(pl.multiple_of(other*384+p*96,16),96)
            downl[rows,0:128]=v[192:288].astype(BF)
            downl[rows,128:192]=v[288:384][:,:64].astype(BF)
        outwl[half(other,128),:]=jnp.concatenate([jnp.concatenate([goutl[0:96],gdnl[0:96,0:64]],1).astype(BF),jnp.zeros((32,192),BF)],0)
    def load_bias():
        v=column(19)
        for j in range(12):
            upb[:,pl.ds(pl.multiple_of(other*1536+128*j,128),128)]=v[384+j:385+j]
        for j in range(3):
            upbl[:,pl.ds(pl.multiple_of(other*384+128*j,128),128)]=v[396+j:397+j]
    @pl.when(first)
    def _():
        three[0][4].wait()
        load_bias()
        upb[:,half(mp,1536)]=upb_own[...]; upbl[:,half(mp,384)]=upbl_own[...]
    def hook():
        @pl.when(first)
        def _():
            own[2].wait()
            outwl[half(mp,128),:]=jnp.concatenate([outl_own[...],jnp.zeros((32,192),BF)],0)
            upl[:,half(mp,384)]=upl_own[...]
            downl[half(mp,384),:]=downl_own[...]
            for i,cps in enumerate(three):
                for k,cp in enumerate(cps):
                    if (i,k)!=(0,4): cp.wait()
                p=s_ref[2+i]
                base=16+4*i if i<3 else 0
                for j in range(6):
                    down[pl.ds(pl.multiple_of(other*1536+p*384,16),384),128*j:128*j+128]=column(base+j//2)[384*(j%2):384*(j%2)+384].astype(BF)
            unpack_small()
    def both(a,b):
        a=a[...]; b=b[...]
        z=mp==0
        return jnp.concatenate([jnp.where(z,a,b),jnp.where(z,b,a)],1)
    gup=acc.at[:,0:1536]; gdn=acc.at[:,1536:3072]; gout=acc.at[:,3072:3456]
    stream(None,mp*1536,xt[...],both(oa,ob),oa[...],ct[...],outw,up,down,sh,ga,upb,act,gp,to,dr1,dos,gup,gdn,gout,st,bst,first,512,tm[...],hook)
    stream(None,mp*384,xl[...],both(ola,olb),ola[...],cl[...].T,outwl,upl,downl,shl,gal,upbl,actl,gpl,lo,dr1l,dosl,gupl,gdnl,goutl,stl,bstl,first,768,lm[...],None)
    @pl.when(pl.program_id(0)==pl.num_programs(0)-1)
    def _():
        blocks=[gupl[:,128*j:128*j+128] for j in range(3)]+[gdnl[:,128*j:128*j+128] for j in range(3)]+[goutl[...]]
        rest=[st[:,128*j:128*j+128] for j in range(6)]+[bst[:,128*j:128*j+128] for j in range(12)]+[stl[:,0:128]]
        rest+=[jnp.concatenate([stl[:,128:192],jnp.zeros((8,64),F32)],1)]+[bstl[:,128*j:128*j+128] for j in range(3)]+[jnp.zeros((8,128),F32)]
        blocks.append(jnp.concatenate(rest,0))
        for i,v in enumerate(blocks):
            acc[192*(i%4):192*(i%4)+192,3456+128*(i//4):3584+128*(i//4)]=v
        place_blocks(acc,keep,send,sem,s_ref[1],n)


def ffn(n,scal,rowed,params,own,second,third,tile=384):
    rows=rowed[0].shape[0]
    rb=lambda a: pl.BlockSpec((tile,a.shape[1]),lambda p,*_:(p,0))
    full=lambda a: pl.BlockSpec(a.shape,lambda p,*_:(0,)*len(a.shape),pipeline_mode=pl.Buffered(1))
    whole=pl.BlockSpec(memory_space=pl.ANY)
    S=jax.ShapeDtypeStruct
    rowout=[S((rows,768),F32),S((192,rows),F32),S((rows,768),F32),S((rows,192),F32)]
    outspecs=[rb(rowout[0]),pl.BlockSpec((192,tile),lambda p,*_:(0,p)),rb(rowout[2]),rb(rowout[3])]
    dos=[S((2,rows,384),BF),S((2,rows,128),BF)]
    big=block_shapes(768,3712,n)
    V=pltpu.VMEM
    small=[V(a,F32) for a in ((8,768),(8,1536),(192,384),(192,384),(192,128),(8,192),(8,384))]
    weights=[V((768,3072),BF),V((768,768),BF),V((3072,768),BF),V((256,192),BF),V((192,768),BF),V((768,192),BF),V((1,3072),F32),V((1,768),F32)]
    return pl.pallas_call(functools.partial(ffn_kernel,n),
        grid_spec=pltpu.PrefetchScalarGridSpec(num_scalar_prefetch=1,grid=(rows//tile,),
            in_specs=[rb(a) if a.shape[0]==rows else pl.BlockSpec((a.shape[0],tile),lambda p,*_:(0,p)) for a in rowed]+[full(w) for w in params]+[whole]*3+[full(w) for w in own[3:]]+[whole]*16,
            out_specs=outspecs+[pl.BlockSpec((2,tile,a.shape[2]),lambda p,*_:(0,p,0)) for a in dos]+[whole,whole],
            scratch_shapes=[V((tile,3072),BF),V((tile,3072),BF),V((tile,768),BF),V((tile,768),BF),V((768,3712),F32)]+weights+small
                +[pltpu.SemaphoreType.DMA,pltpu.SemaphoreType.DMA((3,)),pltpu.SemaphoreType.DMA((8,2)),pltpu.SemaphoreType.DMA((4,5))]),
        out_shape=rowout+dos+big,
        compiler_params=pltpu.CompilerParams(vmem_limit_bytes=VLIM),cost_estimate=cost(80),name="middle")(scal,*rowed,*params,*own,*second,*[v for pair in third for v in pair])


from jax.sharding import PartitionSpec as P


def pack_kernel(idx_ref, *refs):
    out=refs[-1]
    out[...]=jnp.zeros_like(out)
    r=0
    for src in refs[:-1]:
        lead=src.shape[0] if len(src.shape)==3 else None
        for c in range(lead or 1):
            w=src[c] if lead else src[...]
            n,m=w.shape
            for j in range(0,m,128):
                e=min(128,m-j)
                out[r:r+n,:e]=w[:,j:j+e].astype(F32)
                r+=n


def pack(idx, split, whole, parts, part=(0,1)):
    specs=[]; n=0
    for k,a in enumerate(split):
        rows=a.shape[-2]//parts
        width=a.shape[-1]//(part[1] if k==0 else 1)
        blocks=-(-width//128)
        if a.ndim==3:
            specs.append(pl.BlockSpec((a.shape[0],rows,a.shape[2]),lambda i,s:(0,s[0],0)))
            n+=a.shape[0]*rows*blocks
        else:
            specs.append(pl.BlockSpec((rows,width),functools.partial(lambda c,i,s:(s[0],c),part[0] if k==0 else 0)))
            n+=rows*blocks
    for a in whole:
        specs.append(pl.BlockSpec(a.shape,lambda i,s:(0,0)))
        n+=a.shape[0]*(-(-a.shape[1]//128))
    n=-(-n//8)*8
    return pl.pallas_call(pack_kernel,
        grid_spec=pltpu.PrefetchScalarGridSpec(num_scalar_prefetch=1,grid=(1,),in_specs=specs,
            out_specs=pl.BlockSpec((n,128),lambda i,s:(0,0))),
        out_shape=jax.ShapeDtypeStruct((n,128),F32),
        compiler_params=pltpu.CompilerParams(vmem_limit_bytes=VLIM),cost_estimate=cost(2),name="pack")(idx,*split,*whole)


def unpack_first_kernel(s_ref, pa, pb, pc, pd, wt_own, wl_own, wt, wl, bt, bl):
    mine=s_ref[0]; other=1-mine
    wl[...]=jnp.zeros_like(wl)
    wt[mine]=wt_own[...]
    wl[mine]=wl_own[...]
    bt[...]=jnp.zeros_like(bt); bl[...]=jnp.zeros_like(bl)
    for p,ref in enumerate((pa,pb,pc,pd)):
        i=s_ref[2+p]
        at=lambda n: pl.ds(pl.multiple_of(i*n,n),n)
        r=0
        for c in range(3):
            for j in range(3):
                wt[other,c,at(192),128*j:128*j+128]=ref[r:r+192].astype(BF); r+=192
        for c in range(3):
            wl[other,c,at(48),:]=ref[r:r+48].astype(BF); r+=48
        if p==0:
            for c in range(2):
                for j in range(3):
                    bt[2*c:2*c+1,128*j:128*j+128]=ref[r+2*j+c:r+2*j+c+1]
            r+=6
            for c in range(2):
                bl[2*c:2*c+1,:]=ref[r+c:r+c+1]


def unpack_first(scal, pieces, wt, wl):
    S=jax.ShapeDtypeStruct
    full=lambda a: pl.BlockSpec(a.shape,lambda i,*_:(0,)*len(a.shape))
    outs=[S((2,3,768,384),BF),S((2,3,192,128),BF),S((3,384),F32),S((3,128),F32)]
    ins=[*pieces,wt,wl]
    return pl.pallas_call(unpack_first_kernel,
        grid_spec=pltpu.PrefetchScalarGridSpec(num_scalar_prefetch=1,grid=(1,),in_specs=[full(a) for a in ins],
            out_specs=[full(a) for a in outs]),
        out_shape=outs,compiler_params=pltpu.CompilerParams(vmem_limit_bytes=VLIM),cost_estimate=cost(4),name="unpack")(scal,*ins)


def flip(n, bit):
    return [(i,i^bit) for i in range(n)]


def cross(n, even, odd):
    return [(i,i^(even if i%2==0 else odd)) for i in range(n)]


def gather4(piece, n):
    a=lax.ppermute(piece,"mp",[(0,1),(1,0)])
    b=lax.ppermute(a,"dp",cross(n,2,4))
    c=lax.ppermute(a,"dp",flip(n,1))
    d=lax.ppermute(b,"dp",flip(n,1))
    return a,b,c,d


def gather8(piece, n):
    a=lax.ppermute(piece,"mp",[(0,1),(1,0)])
    b=lax.ppermute(a,"dp",cross(n,2,4))
    e=lax.ppermute(a,"dp",cross(n,4,2))
    f=lax.ppermute(b,"dp",cross(n,4,2))
    return (a,b,e,f)+tuple(lax.ppermute(v,"dp",flip(n,1)) for v in (a,b,e,f))


def ids8(dp):
    base=dp&7; odd=dp&1
    near=jnp.where(odd==0,2,4); far=6-near
    return [base,base^near,base^far,base^6,base^1,base^1^far,base^1^near,base^7]


def join(*values):
    return lax.optimization_barrier(values)


def stages(n):
    return (flip(n,1),cross(n,2,4),cross(n,4,2),flip(n,8))


def halve(keep, recv):
    half=keep.shape[0]//2
    return keep[:half]+recv[:half],keep[half:]+recv[half:]


def bias_rows(pair):
    b=pair.astype(F32)
    return jnp.stack([b[0],jnp.zeros_like(b[0]),b[1]])


def shards(text_in, layout_in, token_mask, box_mask, lengths, text_mask_vec, layout_mask_vec,
           text_qkv, text_qv_bias, text_out_w, text_shifts, text_gains, text_up, text_up_bias, text_down,
           layout_qkv, layout_qv_bias, layout_out_w, layout_shifts, layout_gains, layout_up, layout_up_bias, layout_down,
           text_cot, layout_cot):
    n=lax.axis_size("dp")
    mp=lax.axis_index("mp").astype(jnp.int32); dp=lax.axis_index("dp").astype(jnp.int32)
    core=dp&1; color=((dp>>1)^(dp>>2))&1
    ids=[2*color+core,2*(1-color)+core,2*color+1-core,2*(1-color)+1-core]
    scal=jnp.stack([mp,dp]+ids+ids8(dp))
    idx=ids[0][None]; idx8=(dp&7)[None]
    even_odd=cross(n,2,4); odd_even=cross(n,4,2); core_flip=flip(n,1)
    over=lambda v: lax.ppermute(v,"mp",[(0,1),(1,0)])
    send=lambda v,pairs: lax.ppermute(v,"dp",pairs)
    upb=text_up_bias.astype(F32)[None]; upbl=layout_up_bias.astype(F32)[None]
    p1=pack(idx,[text_qkv,layout_qkv],[text_qv_bias,layout_qv_bias],4)
    p2=pack(idx8,[text_up,text_out_w],[],8)
    p3=pack(idx,[text_down],[],4,(0,2))
    p4=pack(idx,[text_down,layout_out_w,layout_up,layout_down],[upb,upbl],4,(1,2))
    tm=token_mask[:,None]; lm=box_mask[:,None]
    xt=jnp.where(tm==1,text_mask_vec[None],text_in)
    xl=jnp.where(lm==1,layout_mask_vec[None],layout_in)
    sel=jnp.concatenate([jnp.ones_like(token_mask)[None],(token_mask==1).astype(jnp.int32)[None],(box_mask==1).astype(jnp.int32)[None],
        jnp.zeros((5,token_mask.shape[0]),jnp.int32)],0).astype(BF)
    pad=lambda v: jnp.pad(v,((0,0),)*(v.ndim-1)+((0,32),))
    wl=pad(layout_qkv)
    a1=over(p1); a2=over(p2)
    bt=bias_rows(text_qv_bias); bl=pad(bias_rows(layout_qv_bias))
    pages=lengths.shape[0]
    xa,p3,tm,lm,sel=join(xt,p3,tm,lm,sel)
    forward=lambda first,count,x,w,prev: attn_fwd(first,count,lengths,1-mp[None],x,xl,*w,prev)
    w_own=(text_qkv,wl,bt,bl)
    own=forward(0,1,xa,w_own,())
    own,a1,p3=join(own,a1,p3)
    b1=send(a1,even_odd); c1=send(a1,core_flip); a3=over(p3)
    own=forward(1,pages-1,xt,w_own,own)
    own,b1,c1,a2,p4=join(own,b1,c1,a2,p4)
    d1=send(b1,core_flip); b2=send(a2,even_odd); a4=over(p4)
    wt_both,wl_both,bt_o,bl_o=unpack_first(scal,(a1,b1,c1,d1),text_qkv,wl)
    wt_both,wl_both,bt_o,bl_o,a2=join(wt_both,wl_both,bt_o,bl_o,a2)
    e2=send(a2,odd_even)
    w_oth=(wt_both,wl_both,bt_o,bl_o)
    oth=forward(0,1,xt,w_oth,())
    oth,b2,e2,a3=join(oth,b2,e2,a3)
    f2=send(b2,odd_even); b3=send(a3,even_odd); c3=send(a3,core_flip)
    oth=forward(1,pages-1,xt,w_oth,oth)
    oth,f2,b3,c3,a4=join(oth,f2,b3,c3,a4)
    b4=send(a4,even_odd); c4=send(a4,core_flip)
    second=(a2,b2,e2,f2)+tuple(send(v,core_flip) for v in (a2,b2,e2,f2))
    d3=send(b3,core_flip); d4=send(b4,core_flip)
    (to,lo,dr1,dr1l,dO,dOl,keep,out)=ffn(n,scal,[xt,xl,own[6],oth[6],own[7],oth[7],text_cot,layout_cot.T,tm,lm],
        [v.astype(F32) for v in (text_shifts,text_gains,layout_shifts,layout_gains)],
        [text_up,text_out_w,text_down,layout_out_w,layout_up,layout_down,upb,upbl],second,((a3,a4),(b3,b4),(c3,c4),(d3,d4)))
    steps=stages(n)
    wts=[wt_both,wl_both]
    tile=text_in.shape[0]//4
    mine_p=lambda p,c,d: attn_bwd(p,c,lengths,mp[None],own,dO,dOl,d)
    other_p=lambda p,d: attn_bwd(p,1,lengths,1-mp[None],oth,dO,dOl,d)
    sums=lambda d: qkv_grad(n,jnp.stack([mp,dp]),pages,xt,xl,*d,sel,*wts)
    inputs=lambda d: input_grad(tile,d,wts,dr1,dr1l,tm,lm)
    if n==16:
        out=send(out,steps[0])
        d_own=mine_p(0,1,())
        d_own,out,keep=join(d_own,out,keep)
        keep,out=halve(keep,out)
        out=send(out,steps[1])
        d_own=mine_p(1,pages-1,d_own)
        qkeep,qout=sums(d_own)
        qkeep,qout,keep,out=join(qkeep,qout,keep,out)
        qout=send(qout,steps[0])
        keep,out=halve(keep,out)
        out=send(out,steps[2])
        d_oth=other_p(0,d_own)
        d_oth,qkeep,qout,keep,out=join(d_oth,qkeep,qout,keep,out)
        keep,out=halve(keep,out)
        qkeep,qout=halve(qkeep,qout)
        half=keep.shape[0]//2
        outs=[send(out[:half],steps[3]),out[half:]]
        qout=send(qout,steps[1])
        d_oth=other_p(1,d_oth)
        d_oth,qkeep,qout,outs[0],outs[1]=join(d_oth,qkeep,qout,*outs)
        outs[1]=send(outs[1],steps[3])
        qkeep,qout=halve(qkeep,qout)
        qout=send(qout,steps[2])
        d_oth=other_p(2,d_oth)
        d_oth,qkeep,qout,outs[1]=join(d_oth,qkeep,qout,outs[1])
        qkeep,qout=halve(qkeep,qout)
        qout=send(qout,steps[3])
        g=keep+jnp.concatenate(outs,0)
        d_in=inputs(d_oth)
        d_in,qkeep,qout=join(d_in,qkeep,qout)
        qg=qkeep+qout
        small=jnp.concatenate([g[:,3456:],qg[:,1152:]],1)[None]
        for bit in (8,2,4,1):
            got=send(small,flip(n,bit))
            low=(dp&bit)==0
            small=jnp.stack([jnp.where(low,small,got),jnp.where(low,got,small)])
        small=small.reshape(2,2,2,2,-1,384).transpose(3,1,2,0,4,5).reshape(-1,384)
    else:
        d_own=mine_p(0,pages,())
        qkeep,qout=sums(d_own)
        rs=lambda v: lax.psum_scatter(v,"dp",scatter_dimension=0,tiled=True)
        g=rs(keep); qg=rs(qkeep)
        d_oth=d_own
        for p in range(pages): d_oth=other_p(p,d_oth)
        d_in=inputs(d_oth)
        small=lax.all_gather(jnp.concatenate([g[:,3456:],qg[:,1152:]],1),"dp",tiled=True)
    tg,lg=d_in
    r=g.shape[0]
    early=small[:,:256]; mine=small[:,256:]
    block=lambda i: early[192*(i%4):192*(i%4)+192,128*(i//4):128*(i//4)+128]
    wide=lambda v,r,k: jnp.concatenate([v[r+8*j:r+8*j+8] for j in range(k)],1)
    gupl=jnp.concatenate([block(j) for j in range(3)],1); gdnl=jnp.concatenate([block(3+j) for j in range(3)],1)
    rest=block(7)
    st=wide(rest,0,6); bst=wide(rest,48,12); stl=wide(rest,144,2)[:,:192]; bstl=wide(rest,160,3)
    sums=mine[576:]
    cs=jnp.stack([wide(sums,32*c,3)[0] for c in (0,2)]); csl=jnp.stack([sums[32*c+24,:96] for c in (0,2)])
    vec=jnp.concatenate([wide(sums,96,6)[1],wide(sums,144,2)[2,:192]])[None]
    vec=vec+over(vec)
    tvec=vec[0,:768]+st[6]; lvec=vec[0,768:]+stl[6]
    qgl=jnp.stack([mine[192*c:192*c+192,:96] for c in range(3)])
    qg=jnp.moveaxis(qg[:,:1152].reshape(r,3,384),1,0)
    return (to,lo.T,tg,lg.T,tvec,lvec,qg,cs,g[:,3072:3456].T,st[:4],st[4:6],g[:,:1536],bst[0],g[:,1536:3072].T,
            qgl,csl,block(6)[:,:96].T,stl[:4],stl[4:6],gupl,bstl[0],gdnl.T)


def solution(mesh):
    rows=P("dp",None); cols=P(None,"mp"); lead=P("mp",None); cube=P(None,None,"mp")
    weights=(cube,cols,lead,P(),P(),cols,P("mp"),lead)
    return jax.shard_map(shards,mesh=mesh,
        in_specs=(rows,rows,P("dp"),P("dp"),P("dp"),P(),P())+weights+weights+(rows,rows),
        out_specs=(rows,rows,rows,rows,P(),P(),P(None,"dp","mp"),cols,P("mp","dp"),P(),P(),P("dp","mp"),P("mp"),P("mp","dp"),
                   cube,cols,lead,P(),P(),cols,P("mp"),lead),
        check_vma=False)
```

time: 703 us -> 392 us (0.56)
  waiting for transfers between devices: 349 us -> 57.3 us
  blocking collectives: 63.9 us -> 0 us
  Pallas kernels: 199 us -> 247 us
  starting transfers between devices: 10.6 us -> 33.6 us
  other arithmetic: 11.6 us -> 29.5 us
  matrix products: 16.7 us -> 0 us
  local copies, waits for them, and re-layouts: 33.4 us -> 18.4 us
  between operations: 15.2 us -> 1.75 us
    reduce_scatter x3 -> x0, waiting for transfers between devices: 217 us -> none  [shards(): lax.psum_scatter(v, 'dp', scatter_dimension=v.ndim - 2, tiled=True)]
    psum x1 -> x0, blocking collectives: 63.9 us -> none  [shards(): lax.psum((qgl, goutl[:, :96].T, gupl, gdnl.T, cs[0::2], csl[0::2], bst[0]...]
    ppermute x16 -> x34, waiting for transfers between devices: 110 us -> 57.3 us  [the longest x29 46 us: shards(): send = lambda v, pairs: lax.ppermute(v, 'dp', pairs)]
    pallas_call x8 -> x12, Pallas kernels: 186 us -> 233 us  [the longest x1 104 us: ffn(): pl.pallas_call(functools.partial(ffn_kernel, n), grid_spec=pltpu.Prefetch...]
    ppermute x16 -> x34, starting transfers between devices: 10.5 us -> 33.6 us  [the longest x29 25.3 us: shards(): send = lambda v, pairs: lax.ppermute(v, 'dp', pairs)]
    unnamed x5 -> x0, waiting for transfers between devices: 21.9 us -> none
    add x0 -> x11, other arithmetic: none -> 17.3 us  [the longest x6 15 us: halve(): return (keep[:half] + recv[:half], keep[half:] + recv[half:])]
    dot_general x6 -> x0, matrix products: 16.7 us -> none  [the longest x4 8.67 us: shards(): jnp.einsum('cne,cde->nd', d, w, preferred_element_type=F32)]
  transfers between devices with their start and end apart: 20 -> 34, of which waited for: 9 -> 12; matrix products, arithmetic and copies ran while one was open for 5% -> 7% of each run, Pallas kernels for 12% -> 36%
where the time goes in v2:
time: 392 us; the launch traced here: 387 us
  Pallas kernels  247 us (63%)
  waiting for transfers between devices  57.3 us (15%)
  starting transfers between devices  33.6 us (9%)
  other arithmetic  29.5 us (8%)
  local copies, waits for them, and re-layouts  18.4 us (5%)
    pallas_call x1, Pallas kernels, ffn(): pl.pallas_call(functools.partial(ffn_kernel, n), grid_spec=pltpu.Prefetch...  104 us
    pallas_call x5, Pallas kernels, attn_bwd(): pl.pallas_call(functools.partial(bwd_kernel, first), grid_spec=pltpu.Pref...  59.1 us
    ppermute x29, waiting for transfers between devices, shards(): send = lambda v, pairs: lax.ppermute(v, 'dp', pairs)  46 us
    pallas_call x4, Pallas kernels, attn_fwd(): pl.pallas_call(functools.partial(attn_fwd_kernel, first), grid_spec=pltpu...  44 us
    ppermute x29, starting transfers between devices, shards(): send = lambda v, pairs: lax.ppermute(v, 'dp', pairs)  25.3 us
    add x6, other arithmetic, halve(): return (keep[:half] + recv[:half], keep[half:] + recv[half:])  15 us
    pallas_call x1, Pallas kernels, input_grad(): pl.pallas_call(dx_kernel, grid=(rows // tile,), in_specs=[pb(384), pb(128...  13 us
    pallas_call x1, Pallas kernels, qkv_grad(): pl.pallas_call(functools.partial(qkv_grad_kernel, n), grid_spec=pltpu.Pre...  12.6 us
  transfers between devices with their start and end apart: 34, of which 12 were waited for; matrix products, arithmetic and copies ran while one was open for 7% of the time, Pallas kernels for 36%

profile of v2, /device:TPU:0, one launch (start us, length us, event | category | flops | bytes accessed | tf_op | source)
XLA Modules:
  0.0 387.1 jit_solution(18416799072977308526)
XLA Ops:
  0.7 2.2 pack.5
  2.9 3.0 collective-permute-start
  13.9 8.3 %attn_fwd.4 = (bf16[1536,384]{1,0:T(8,128)(2,1)}, bf16[1536,384]{1,0:T(8,128)(2,1)}, bf16[1536,384]{1,0:T(8,128)(2,1)}, bf16[1536,128]{1,0:T(8,128)(2,1)}, bf16[...) custom-call(s32[3]{0:T(128)} %len_ref.17, ...), custom_call_target="tpu_custom_call" | custom-call | flops 62000000 | bytes 1024 | tf_op jit(solution)/shard_map/attn_fwd/pallas_call | solution.py:63
  22.1 5.3 %collective-permute-done.pa = f32[1880,128]{1,0:T(8,128)S(1)} collective-permute-done((f32[1880,128]{1,0:T(8,128)}, f32[1880,128]{1,0:T(8,128)S(1)}, u32[]{:S(2)}, u32[]{:S(2)}) %collective-permute-start) | collective-permute-done | bytes 962592 | tf_op jit(solution)/shard_map/ppermute | solution.py:582
  36.6 13.8 %attn_fwd.5 = (bf16[1536,384]{1,0:T(8,128)(2,1)}, bf16[1536,384]{1,0:T(8,128)(2,1)}, bf16[1536,384]{1,0:T(8,128)(2,1)}, bf16[1536,128]{1,0:T(8,128)(2,1)}, bf16[...) custom-call(s32[3]{0:T(128)} %len_ref.17, ...), custom_call_target="tpu_custom_call", output_to_operand_aliasing={{0}: (8, {}), {1}: (9, {}), {2}: (10, {}), {3}: (11, {}), {... | custom-call | flops 124000000 | bytes 1024 | tf_op jit(solution)/shard_map/attn_fwd/pallas_call | solution.py:63
  53.9 5.5 %unpack.1 = (bf16[2,3,768,384]{3,2,1,0:T(8,128)(2,1)}, bf16[2,3,192,128]{3,2,1,0:T(8,128)(2,1)}, f32[3,384]{1,0:T(4,128)}, f32[3,128]{1,0:T(4,128)}) custom-call(s32[14]{0:T(128)} %stack.124.s_ref, f32[1880,128]{1,0:T(8,128)} %copy-done.6, f32[1880,128]{1,0:T(8,128)} %copy-done.7, f32[1880,128]{1,0:T(8,128)} %collective-permute-done.2.pc, ...), custom_call_target="tpu_custom_call" | custom-call | flops 40000000 | bytes 1024 | tf_op jit(solution)/shard_map/unpack/pallas_call | solution.py:517
  63.1 8.4 %attn_fwd.6 = (bf16[1536,384]{1,0:T(8,128)(2,1)}, bf16[1536,384]{1,0:T(8,128)(2,1)}, bf16[1536,384]{1,0:T(8,128)(2,1)}, bf16[1536,128]{1,0:T(8,128)(2,1)}, bf16[...) custom-call(s32[3]{0:T(128)} %len_ref.17, ...), custom_call_target="tpu_custom_call" | custom-call | flops 62000000 | bytes 1024 | tf_op jit(solution)/shard_map/attn_fwd/pallas_call | solution.py:63
  71.5 6.0 %collective-permute-done.7.refs_30_ = f32[1152,128]{1,0:T(8,128)S(1)} collective-permute-done((f32[1152,128]{1,0:T(8,128)}, f32[1152,128]{1,0:T(8,128)S(1)}, u32[]{:S(2)}, u32[]{:S(2)}) %collective-permute-start.7) | collective-permute-done | bytes 589856 | tf_op jit(solution)/shard_map/ppermute | solution.py:582
  79.3 13.6 %attn_fwd.7 = (bf16[1536,384]{1,0:T(8,128)(2,1)}, bf16[1536,384]{1,0:T(8,128)(2,1)}, bf16[1536,384]{1,0:T(8,128)(2,1)}, bf16[1536,128]{1,0:T(8,128)(2,1)}, bf16[...) custom-call(s32[3]{0:T(128)} %len_ref.17, ...), custom_call_target="tpu_custom_call", output_to_operand_aliasing={{0}: (8, {}), {1}: (9, {}), {2}: (10, {}), {3}: (11, {}), {... | custom-call | flops 124000000 | bytes 1024 | tf_op jit(solution)/shard_map/attn_fwd/pallas_call | solution.py:63
  93.0 3.3 collective-permute-done.8.refs_25_
  97.3 11.0 %collective-permute-done.16.refs_33_ = f32[1552,128]{1,0:T(8,128)S(1)} collective-permute-done((f32[1552,128]{1,0:T(8,128)S(1)}, f32[1552,128]{1,0:T(8,128)S(1)}, u32[]{:S(2)}, u32[]{:S(2)}) %collective-permute-start.16) | collective-permute-done | bytes 794656 | tf_op jit(solution)/shard_map/ppermute | solution.py:583
  115.4 104.3 %middle.1 = (f32[1536,768]{1,0:T(8,128)}, f32[192,1536]{1,0:T(8,128)}, f32[1536,768]{1,0:T(8,128)}, f32[1536,192]{1,0:T(8,128)}, bf16[2,1536,384]{2,1,0:T(8,128)...) custom-call(s32[14]{0:T(128)} %stack.124.s_ref, ...), custom_call_target="tpu_custom_call" | custom-call | flops 800000000 | bytes 1024 | tf_op jit(solution)/shard_map/middle/pallas_call | solution.py:437
  219.8 10.4 %attn_bwd.5 = (bf16[6,1536,384]{2,1,0:T(8,128)(2,1)}, bf16[6,1536,128]{2,1,0:T(8,128)(2,1)}) custom-call(s32[3]{0:T(128)} %len_ref.17, s32[1]{0:T(128)} %bitcast.half_ref, bf16[1536,384]{1,0:T(8,128)(2,1)} %get-tuple-element.267.qt, bf16[1536,384]{1,0:T(8,128)(2,1)} %get-tuple-element.268.kt, bf16[1536,384]{1,0:T(8,128)(2,1)} %get-tuple-element.269.vt, ...), custom_call_target="tpu_custom_call" | custom-call | flops 90000000 | bytes 1024 | tf_op jit(solution)/shard_map/attn_bwd/pallas_call | solution.py:160
  230.2 6.5 %slice_add_fusion = (f32[192,3712]{1,0:T(8,128)}, f32[192,3712]{1,0:T(8,128)S(1)}) fusion(f32[384,3712]{1,0:T(8,128)} %collective-permute-done.20, f32[384,3712]{1,0:T(8,128)} %get-tuple-element.287), kind=kLoop, calls=%fused_computation | loop fusion | flops 1425408 | bytes 17104896 | tf_op jit(solution)/shard_map/add | solution.py:563
  237.7 17.4 %attn_bwd.6 = (bf16[6,1536,384]{2,1,0:T(8,128)(2,1)}, bf16[6,1536,128]{2,1,0:T(8,128)(2,1)}) custom-call(s32[3]{0:T(128)} %len_ref.17, s32[1]{0:T(128)} %bitcast.half_ref, bf16[1536,384]{1,0:T(8,128)(2,1)} %get-tuple-element.267.qt, bf16[1536,384]{1,0:T(8,128)(2,1)} %get-tuple-element.268.kt, ...), custom_call_target="tpu_custom_call", output_to_operand_aliasing={{0}: (13, {}), {1}: (14, {})} | custom-call | flops 180000000 | bytes 1024 | tf_op jit(solution)/shard_map/attn_bwd/pallas_call | solution.py:160
  255.2 12.6 %qkv_grad.1 = (f32[384,1280]{1,0:T(8,128)}, f32[384,1280]{1,0:T(8,128)}) custom-call(s32[2]{0:T(128)} %pad_add_fusion.pos_ref, bf16[1536,768]{1,0:T(8,128)(2,1)} %broadcast_select_fusion.xt_ref.refs_0_.xt, bf16[1536,192]{1,0:T(8,128)(2,1)} %broadcast_select_fusion.1.xl_ref.refs_1_.xl, bf16[6,1536,384]{2,1,0:T(8,128)(2,1)} %get-tuple-element.280.rest_0_.dpt, ...), custom_call_target="tpu_custom_call" | custom-call | flops 80000000 | bytes 1024 | tf_op jit(solution)/shard_map/qkv_grad/pallas_call | solution.py:257
  267.8 3.3 collective-permute-done.21
  271.0 3.7 slice_add_fusion.2
  275.2 10.3 %attn_bwd.7 = (bf16[6,1536,384]{2,1,0:T(8,128)(2,1)}, bf16[6,1536,128]{2,1,0:T(8,128)(2,1)}) custom-call(s32[3]{0:T(128)} %len_ref.17, s32[1]{0:T(128)S(6)} %sub.26.half_ref, bf16[1536,384]{1,0:T(8,128)(2,1)} %get-tuple-element.258.qt, bf16[1536,384]{1,0:T(8,128)(2,1)} %get-tuple-element.259.kt, ...), custom_call_target="tpu_custom_call", output_to_operand_aliasing={{0}: (13, {}), {1}: (14, {})} | custom-call | flops 90000000 | bytes 1024 | tf_op jit(solution)/shard_map/attn_bwd/pallas_call | solution.py:160
  285.5 8.2 %collective-permute-done.23 = f32[96,3712]{1,0:T(8,128)S(1)} collective-permute-done((f32[96,3712]{1,0:T(8,128)}, f32[96,3712]{1,0:T(8,128)S(1)}, u32[]{:S(2)}, u32[]{:S(2)}) %collective-permute-start.23) | collective-permute-done | bytes 1425440 | tf_op jit(solution)/shard_map/ppermute | solution.py:583
  294.9 3.4 slice_add_fusion.4
  299.8 2.6 collective-permute-start.25
  302.4 10.7 %attn_bwd.8 = (bf16[6,1536,384]{2,1,0:T(8,128)(2,1)}, bf16[6,1536,128]{2,1,0:T(8,128)(2,1)}) custom-call(s32[3]{0:T(128)} %len_ref.17, s32[1]{0:T(128)S(6)} %sub.26.half_ref, bf16[1536,384]{1,0:T(8,128)(2,1)} %get-tuple-element.258.qt, bf16[1536,384]{1,0:T(8,128)(2,1)} %get-tuple-element.259.kt, ...), custom_call_target="tpu_custom_call", output_to_operand_aliasing={{0}: (13, {}), {1}: (14, {})} | custom-call | flops 90000000 | bytes 1024 | tf_op jit(solution)/shard_map/attn_bwd/pallas_call | solution.py:160
  316.6 4.8 %collective-permute-start.26 = (f32[96,1280]{1,0:T(8,128)S(1)}, f32[96,1280]{1,0:T(8,128)S(1)}, u32[]{:S(2)}, u32[]{:S(2)}) collective-permute-start(f32[96,1280]{1,0:T(8,128)S(1)} %get-tuple-element.376), channel_id=1, source_target_pairs={{0,8},{2,6},{4,12},{6,2},{8,0},{10,14},{12,4},{14,10},{16,24},{18,... | collective-permute-start | bytes 1474568 | tf_op jit(solution)/shard_map/ppermute | solution.py:583
  321.4 3.2 collective-permute-start.27
  324.6 10.4 %attn_bwd.9 = (bf16[6,1536,384]{2,1,0:T(8,128)(2,1)}, bf16[6,1536,128]{2,1,0:T(8,128)(2,1)}) custom-call(s32[3]{0:T(128)} %len_ref.17, s32[1]{0:T(128)S(6)} %sub.26.half_ref, bf16[1536,384]{1,0:T(8,128)(2,1)} %get-tuple-element.258.qt, bf16[1536,384]{1,0:T(8,128)(2,1)} %get-tuple-element.259.kt, ...), custom_call_target="tpu_custom_call", output_to_operand_aliasing={{0}: (13, {}), {1}: (14, {})} | custom-call | flops 90000000 | bytes 1024 | tf_op jit(solution)/shard_map/attn_bwd/pallas_call | solution.py:160
  335.0 5.3 %collective-permute-done.27 = f32[24,3712]{1,0:T(8,128)S(1)} collective-permute-done((f32[24,3712]{1,0:T(8,128)}, f32[24,3712]{1,0:T(8,128)S(1)}, u32[]{:S(2)}, u32[]{:S(2)}) %collective-permute-start.27) | collective-permute-done | bytes 356384 | tf_op jit(solution)/shard_map/ppermute | solution.py:583
  342.2 13.0 %input_grad.1 = (f32[1536,768]{1,0:T(8,128)}, f32[192,1536]{1,0:T(8,128)}) custom-call(bf16[6,1536,384]{2,1,0:T(8,128)(2,1)} %get-tuple-element.308.dpt, bf16[6,1536,128]{2,1,0:T(8,128)(2,1)} %get-tuple-element.309.dpl, bf16[2,3,768,384]{3,2,1,0:T(8,128)(2,1)} %get-tuple-element.210.wt_ref.wt, bf16[2,3,192,128]{3,2,1,0:T(8,128)(2,1)} %get-tuple-element.211.wl_ref.wl, ...), custom_call_target="tpu_custom_call" | custom-call | flops 50000000 | bytes 1024 | tf_op jit(solution)/shard_map/input_grad/pallas_call | solution.py:189
  355.3 3.0 collective-permute-start.29
  358.2 3.1 collective-permute-done.29
  362.2 4.5 %collective-permute-done.30 = f32[2,1,48,384]{3,2,0,1:T(8,128)S(1)} collective-permute-done((f32[2,1,48,384]{3,2,0,1:T(8,128)S(1)}, f32[2,1,48,384]{3,2,0,1:T(8,128)S(1)}, u32[]{:S(2)}, u32[]{:S(2)}) %collective-permute-start.30) | collective-permute-done | bytes 147488 | tf_op jit(solution)/shard_map/ppermute | solution.py:583
  368.8 4.7 %collective-permute-done.31 = f32[2,2,1,48,384]{4,3,1,0,2:T(8,128)S(1)} collective-permute-done((f32[2,2,1,48,384]{4,3,1,0,2:T(8,128)S(1)}, f32[2,2,1,48,384]{4,3,1,0,2:T(8,128)S(1)}, u32[]{:S(2)}, u32[]{:S(2)}) %collective-permute-start.31) | collective-permute-done | bytes 294944 | tf_op jit(solution)/shard_map/ppermute | solution.py:583
  (211 shorter events, 59.7 us)
Async XLA Ops:
  2.9 24.5 %collective-permute-start = (f32[1880,128]{1,0:T(8,128)}, f32[1880,128]{1,0:T(8,128)S(1)}, u32[]{:S(2)}, u32[]{:S(2)}) collective-permute-start(f32[1880,128]{1,0:T(8,128)} %pack.5), channel_id=1, source_target_pairs={{0,1},{1,0},{2,3},{3,2},{4,5},{5,4},{6,7},{7,6},{8,9},{9,8},{10,11... | collective-permute-start | bytes 2887688 | tf_op jit(solution)/shard_map/ppermute | solution.py:582
  27.4 23.0 %collective-permute-start.1 = (f32[1880,128]{1,0:T(8,128)S(1)}, f32[1880,128]{1,0:T(8,128)S(1)}, u32[]{:S(2)}, u32[]{:S(2)}) collective-permute-start(f32[1880,128]{1,0:T(8,128)S(1)} %collective-permute-done.pa), channel_id=1, source_target_pairs={{0,4},{2,10},{4,0},{6,14},{8,12},{10,2},{12,8},{14,6},{16,20},{18,... | collective-permute-start | bytes 2887688 | tf_op jit(solution)/shard_map/ppermute | solution.py:583
  29.1 21.3 %collective-permute-start.2 = (f32[1880,128]{1,0:T(8,128)S(1)}, f32[1880,128]{1,0:T(8,128)}, u32[]{:S(2)}, u32[]{:S(2)}) collective-permute-start(f32[1880,128]{1,0:T(8,128)S(1)} %collective-permute-done.pa), channel_id=1, source_target_pairs={{0,2},{2,0},{4,6},{6,4},{8,10},{10,8},{12,14},{14,12},{16,18},{18,... | collective-permute-start | bytes 2887688 | tf_op jit(solution)/shard_map/ppermute | solution.py:583
  31.1 19.3 %collective-permute-start.3 = (f32[1440,128]{1,0:T(8,128)}, f32[1440,128]{1,0:T(8,128)}, u32[]{:S(2)}, u32[]{:S(2)}) collective-permute-start(f32[1440,128]{1,0:T(8,128)} %pack.6), channel_id=1, source_target_pairs={{0,1},{1,0},{2,3},{3,2},{4,5},{5,4},{6,7},{7,6},{8,9},{9,8},{10,11... | collective-permute-start | bytes 2211848 | tf_op jit(solution)/shard_map/ppermute | solution.py:582
  51.3 26.2 %collective-permute-start.5 = (f32[1440,128]{1,0:T(8,128)}, f32[1440,128]{1,0:T(8,128)}, u32[]{:S(2)}, u32[]{:S(2)}) collective-permute-start(f32[1440,128]{1,0:T(8,128)} %collective-permute-done.3.refs_22_), channel_id=1, source_target_pairs={{0,4},{2,10},{4,0},{6,14},{8,12},{10,2},{12,8},{14,6},{16,20},{18,... | collective-permute-start | bytes 2211848 | tf_op jit(solution)/shard_map/ppermute | solution.py:583
  59.5 18.1 %collective-permute-start.6 = (f32[1440,128]{1,0:T(8,128)}, f32[1440,128]{1,0:T(8,128)S(1)}, u32[]{:S(2)}, u32[]{:S(2)}) collective-permute-start(f32[1440,128]{1,0:T(8,128)} %collective-permute-done.3.refs_22_), channel_id=1, source_target_pairs={{0,8},{2,6},{4,12},{6,2},{8,0},{10,14},{12,4},{14,10},{16,24},{18,... | collective-permute-start | bytes 2211848 | tf_op jit(solution)/shard_map/ppermute | solution.py:583
  61.1 16.5 %collective-permute-start.7 = (f32[1152,128]{1,0:T(8,128)}, f32[1152,128]{1,0:T(8,128)S(1)}, u32[]{:S(2)}, u32[]{:S(2)}) collective-permute-start(f32[1152,128]{1,0:T(8,128)} %pack.4), channel_id=1, source_target_pairs={{0,1},{1,0},{2,3},{3,2},{4,5},{5,4},{6,7},{7,6},{8,9},{9,8},{10,11... | collective-permute-start | bytes 1769480 | tf_op jit(solution)/shard_map/ppermute | solution.py:582
  62.5 30.5 %collective-permute-start.11 = (f32[1552,128]{1,0:T(8,128)S(1)}, f32[1552,128]{1,0:T(8,128)S(1)}, u32[]{:S(2)}, u32[]{:S(2)}) collective-permute-start(f32[1552,128]{1,0:T(8,128)S(1)} %copy-done.9), channel_id=1, source_target_pairs={{0,1},{1,0},{2,3},{3,2},{4,5},{5,4},{6,7},{7,6},{8,9},{9,8},{10,11... | collective-permute-start | bytes 2383880 | tf_op jit(solution)/shard_map/ppermute | solution.py:582
  78.4 17.9 %collective-permute-start.8 = (f32[1440,128]{1,0:T(8,128)}, f32[1440,128]{1,0:T(8,128)S(1)}, u32[]{:S(2)}, u32[]{:S(2)}) collective-permute-start(f32[1440,128]{1,0:T(8,128)} %collective-permute-done.5.refs_23_), channel_id=1, source_target_pairs={{0,8},{2,6},{4,12},{6,2},{8,0},{10,14},{12,4},{14,10},{16,24},{18,... | collective-permute-start | bytes 2211848 | tf_op jit(solution)/shard_map/ppermute | solution.py:583
  78.7 14.2 %collective-permute-start.10 = (f32[1152,128]{1,0:T(8,128)}, f32[1152,128]{1,0:T(8,128)}, u32[]{:S(2)}, u32[]{:S(2)}) collective-permute-start(f32[1152,128]{1,0:T(8,128)} %copy-done.16), channel_id=1, source_target_pairs={{0,2},{2,0},{4,6},{6,4},{8,10},{10,8},{12,14},{14,12},{16,18},{18,... | collective-permute-start | bytes 1769480 | tf_op jit(solution)/shard_map/ppermute | solution.py:583
  78.7 14.2 %collective-permute-start.9 = (f32[1152,128]{1,0:T(8,128)}, f32[1152,128]{1,0:T(8,128)}, u32[]{:S(2)}, u32[]{:S(2)}) collective-permute-start(f32[1152,128]{1,0:T(8,128)} %copy-done.16), channel_id=1, source_target_pairs={{0,4},{2,10},{4,0},{6,14},{8,12},{10,2},{12,8},{14,6},{16,20},{18,... | collective-permute-start | bytes 1769480 | tf_op jit(solution)/shard_map/ppermute | solution.py:583
  96.3 12.1 %collective-permute-start.16 = (f32[1552,128]{1,0:T(8,128)S(1)}, f32[1552,128]{1,0:T(8,128)S(1)}, u32[]{:S(2)}, u32[]{:S(2)}) collective-permute-start(f32[1552,128]{1,0:T(8,128)S(1)} %collective-permute-done.11.refs_31_), channel_id=1, source_target_pairs={{0,4},{2,10},{4,0},{6,14},{8,12},{10,2},{12,8},{14,6},{16,20},{18,... | collective-permute-start | bytes 2383880 | tf_op jit(solution)/shard_map/ppermute | solution.py:583
  96.8 12.1 %collective-permute-start.12 = (f32[1440,128]{1,0:T(8,128)}, f32[1440,128]{1,0:T(8,128)}, u32[]{:S(2)}, u32[]{:S(2)}) collective-permute-start(f32[1440,128]{1,0:T(8,128)} %collective-permute-done.3.refs_22_), channel_id=1, source_target_pairs={{0,2},{2,0},{4,6},{6,4},{8,10},{10,8},{12,14},{14,12},{16,18},{18,... | collective-permute-start | bytes 2211848 | tf_op jit(solution)/shard_map/ppermute | solution.py:583
  96.8 12.1 %collective-permute-start.13 = (f32[1440,128]{1,0:T(8,128)}, f32[1440,128]{1,0:T(8,128)}, u32[]{:S(2)}, u32[]{:S(2)}) collective-permute-start(f32[1440,128]{1,0:T(8,128)} %collective-permute-done.5.refs_23_), channel_id=1, source_target_pairs={{0,2},{2,0},{4,6},{6,4},{8,10},{10,8},{12,14},{14,12},{16,18},{18,... | collective-permute-start | bytes 2211848 | tf_op jit(solution)/shard_map/ppermute | solution.py:583
  97.3 16.9 %collective-permute-start.17 = (f32[1552,128]{1,0:T(8,128)S(1)}, f32[1552,128]{1,0:T(8,128)S(1)}, u32[]{:S(2)}, u32[]{:S(2)}) collective-permute-start(f32[1552,128]{1,0:T(8,128)S(1)} %collective-permute-done.11.refs_31_), channel_id=1, source_target_pairs={{0,2},{2,0},{4,6},{6,4},{8,10},{10,8},{12,14},{14,12},{16,18},{18,... | collective-permute-start | bytes 2383880 | tf_op jit(solution)/shard_map/ppermute | solution.py:583
  108.4 5.9 %collective-permute-start.19 = (f32[1552,128]{1,0:T(8,128)S(1)}, f32[1552,128]{1,0:T(8,128)S(1)}, u32[]{:S(2)}, u32[]{:S(2)}) collective-permute-start(f32[1552,128]{1,0:T(8,128)S(1)} %collective-permute-done.16.refs_33_), channel_id=1, source_target_pairs={{0,2},{2,0},{4,6},{6,4},{8,10},{10,8},{12,14},{14,12},{16,18},{18,... | collective-permute-start | bytes 2383880 | tf_op jit(solution)/shard_map/ppermute | solution.py:583
  108.4 5.8 %collective-permute-start.14 = (f32[1440,128]{1,0:T(8,128)}, f32[1440,128]{1,0:T(8,128)}, u32[]{:S(2)}, u32[]{:S(2)}) collective-permute-start(f32[1440,128]{1,0:T(8,128)} %copy-done.14), channel_id=1, source_target_pairs={{0,2},{2,0},{4,6},{6,4},{8,10},{10,8},{12,14},{14,12},{16,18},{18,... | collective-permute-start | bytes 2211848 | tf_op jit(solution)/shard_map/ppermute | solution.py:583
  108.9 5.3 %collective-permute-start.15 = (f32[1440,128]{1,0:T(8,128)}, f32[1440,128]{1,0:T(8,128)}, u32[]{:S(2)}, u32[]{:S(2)}) collective-permute-start(f32[1440,128]{1,0:T(8,128)} %copy-done.15), channel_id=1, source_target_pairs={{0,2},{2,0},{4,6},{6,4},{8,10},{10,8},{12,14},{14,12},{16,18},{18,... | collective-permute-start | bytes 2211848 | tf_op jit(solution)/shard_map/ppermute | solution.py:583
  108.9 5.3 %collective-permute-start.18 = (f32[1152,128]{1,0:T(8,128)}, f32[1152,128]{1,0:T(8,128)}, u32[]{:S(2)}, u32[]{:S(2)}) collective-permute-start(f32[1152,128]{1,0:T(8,128)} %collective-permute-done.9.refs_32_), channel_id=1, source_target_pairs={{0,2},{2,0},{4,6},{6,4},{8,10},{10,8},{12,14},{14,12},{16,18},{18,... | collective-permute-start | bytes 1769480 | tf_op jit(solution)/shard_map/ppermute | solution.py:583
  219.7 10.5 %collective-permute-start.20 = (f32[384,3712]{1,0:T(8,128)}, f32[384,3712]{1,0:T(8,128)}, u32[]{:S(2)}, u32[]{:S(2)}) collective-permute-start(f32[384,3712]{1,0:T(8,128)} %get-tuple-element.276), channel_id=1, source_target_pairs={{0,2},{2,0},{4,6},{6,4},{8,10},{10,8},{12,14},{14,12},{16,18},{18,... | collective-permute-start | bytes 17104904 | tf_op jit(solution)/shard_map/ppermute | solution.py:583
  236.6 34.4 %collective-permute-start.21 = (f32[192,3712]{1,0:T(8,128)}, f32[192,3712]{1,0:T(8,128)}, u32[]{:S(2)}, u32[]{:S(2)}) collective-permute-start(f32[192,3712]{1,0:T(8,128)} %get-tuple-element.370), channel_id=1, source_target_pairs={{0,4},{2,10},{4,0},{6,14},{8,12},{10,2},{12,8},{14,6},{16,20},{18,... | collective-permute-start | bytes 8552456 | tf_op jit(solution)/shard_map/ppermute | solution.py:583
  271.0 22.7 %collective-permute-start.22 = (f32[384,1280]{1,0:T(8,128)}, f32[384,1280]{1,0:T(8,128)}, u32[]{:S(2)}, u32[]{:S(2)}) collective-permute-start(f32[384,1280]{1,0:T(8,128)} %get-tuple-element.290), channel_id=1, source_target_pairs={{0,2},{2,0},{4,6},{6,4},{8,10},{10,8},{12,14},{14,12},{16,18},{18,... | collective-permute-start | bytes 5898248 | tf_op jit(solution)/shard_map/ppermute | solution.py:583
  274.7 19.0 %collective-permute-start.23 = (f32[96,3712]{1,0:T(8,128)}, f32[96,3712]{1,0:T(8,128)S(1)}, u32[]{:S(2)}, u32[]{:S(2)}) collective-permute-start(f32[96,3712]{1,0:T(8,128)} %get-tuple-element.372), channel_id=1, source_target_pairs={{0,8},{2,6},{4,12},{6,2},{8,0},{10,14},{12,4},{14,10},{16,24},{18,... | collective-permute-start | bytes 4276232 | tf_op jit(solution)/shard_map/ppermute | solution.py:583
  298.3 16.1 %collective-permute-start.24 = (f32[192,1280]{1,0:T(8,128)}, f32[192,1280]{1,0:T(8,128)S(1)}, u32[]{:S(2)}, u32[]{:S(2)}) collective-permute-start(f32[192,1280]{1,0:T(8,128)} %get-tuple-element.374), channel_id=1, source_target_pairs={{0,4},{2,10},{4,0},{6,14},{8,12},{10,2},{12,8},{14,6},{16,20},{18,... | collective-permute-start | bytes 2949128 | tf_op jit(solution)/shard_map/ppermute | solution.py:583
  299.8 14.5 %collective-permute-start.25 = (f32[24,3712]{1,0:T(8,128)}, f32[24,3712]{1,0:T(8,128)S(1)}, u32[]{:S(2)}, u32[]{:S(2)}) collective-permute-start(f32[24,3712]{1,0:T(8,128)} %get-tuple-element.426), channel_id=1, source_target_pairs={{0,16},{2,18},{4,20},{6,22},{8,24},{10,26},{12,28},{14,30},{16,0},... | collective-permute-start | bytes 1069064 | tf_op jit(solution)/shard_map/ppermute | solution.py:583
  316.6 23.7 %collective-permute-start.26 = (f32[96,1280]{1,0:T(8,128)S(1)}, f32[96,1280]{1,0:T(8,128)S(1)}, u32[]{:S(2)}, u32[]{:S(2)}) collective-permute-start(f32[96,1280]{1,0:T(8,128)S(1)} %get-tuple-element.376), channel_id=1, source_target_pairs={{0,8},{2,6},{4,12},{6,2},{8,0},{10,14},{12,4},{14,10},{16,24},{18,... | collective-permute-start | bytes 1474568 | tf_op jit(solution)/shard_map/ppermute | solution.py:583
  321.4 18.9 %collective-permute-start.27 = (f32[24,3712]{1,0:T(8,128)}, f32[24,3712]{1,0:T(8,128)S(1)}, u32[]{:S(2)}, u32[]{:S(2)}) collective-permute-start(f32[24,3712]{1,0:T(8,128)} %get-tuple-element.307), channel_id=1, source_target_pairs={{0,16},{2,18},{4,20},{6,22},{8,24},{10,26},{12,28},{14,30},{16,0},... | collective-permute-start | bytes 1069064 | tf_op jit(solution)/shard_map/ppermute | solution.py:583
  341.0 14.1 %collective-permute-start.28 = (f32[48,1280]{1,0:T(8,128)S(1)}, f32[48,1280]{1,0:T(8,128)S(1)}, u32[]{:S(2)}, u32[]{:S(2)}) collective-permute-start(f32[48,1280]{1,0:T(8,128)S(1)} %get-tuple-element.421), channel_id=1, source_target_pairs={{0,16},{2,18},{4,20},{6,22},{8,24},{10,26},{12,28},{14,30},{16,0},... | collective-permute-start | bytes 737288 | tf_op jit(solution)/shard_map/ppermute | solution.py:583
  355.3 6.1 %collective-permute-start.29 = (f32[1,48,384]{2,1,0:T(8,128)S(1)}, f32[1,48,384]{2,1,0:T(8,128)S(1)}, u32[]{:S(2)}, u32[]{:S(2)}) collective-permute-start(f32[1,48,384]{2,1,0:T(8,128)S(1)} %maximum_bitcast_fusion.2), channel_id=1, source_target_pairs={{0,16},{2,18},{4,20},{6,22},{8,24},{10,26},{12,28},{14,30},{16,0},... | collective-permute-start | bytes 221192 | tf_op jit(solution)/shard_map/ppermute | solution.py:583
  361.4 5.2 %collective-permute-start.30 = (f32[2,1,48,384]{3,2,0,1:T(8,128)S(1)}, f32[2,1,48,384]{3,2,0,1:T(8,128)S(1)}, u32[]{:S(2)}, u32[]{:S(2)}) collective-permute-start(f32[2,1,48,384]{3,2,0,1:T(8,128)S(1)} %fusion.5), channel_id=1, source_target_pairs={{0,4},{2,6},{4,0},{6,2},{8,12},{10,14},{12,8},{14,10},{16,20},{18,... | collective-permute-start | bytes 442376 | tf_op jit(solution)/shard_map/ppermute | solution.py:583
  366.7 6.8 %collective-permute-start.31 = (f32[2,2,1,48,384]{4,3,1,0,2:T(8,128)S(1)}, f32[2,2,1,48,384]{4,3,1,0,2:T(8,128)S(1)}, u32[]{:S(2)}, u32[]{:S(2)}) collective-permute-start(f32[2,2,1,48,384]{4,3,1,0,2:T(8,128)S(1)} %fusion.3), channel_id=1, source_target_pairs={{0,8},{2,10},{4,12},{6,14},{8,0},{10,2},{12,4},{14,6},{16,24},{18,... | collective-permute-start | bytes 884744 | tf_op jit(solution)/shard_map/ppermute | solution.py:583
  377.8 7.7 %collective-permute-start.33 = (f32[1,960]{1,0:T(1,128)S(1)}, f32[1,960]{1,0:T(1,128)S(1)}, u32[]{:S(2)}, u32[]{:S(2)}) collective-permute-start(f32[1,960]{1,0:T(1,128)S(1)} %bitcast.112), channel_id=1, source_target_pairs={{0,1},{1,0},{2,3},{3,2},{4,5},{5,4},{6,7},{7,6},{8,9},{9,8},{10,11... | collective-permute-start | bytes 11528 | tf_op jit(solution)/shard_map/ppermute | solution.py:582
  (35 other events, 215.4 us)
